TPU v7x, 256 devices: a whole 4x4x8 slice. The times are simulated.
256 devices in a mesh: prompt: 16 (over z_lo, y), roll: 16 (over z_hi, x, core).
Axes of the slice: x: 4, y: 4, z: 8 (z_hi: 2, z_lo: 4; z = z_hi * 4 + z_lo), core: 2. Of those that a mesh axis runs over, the one named last changes fastest.
Arguments:
- pre_q: bfloat16 [16384, 1024], P(('prompt', 'roll')), parts along dimension 0, may hold values from -8 to 8
- pre_kv: bfloat16 [16384, 256], P(('prompt', 'roll')), parts along dimension 0, may hold values from -8 to 8
- roll_q: bfloat16 [256, 128, 1024], P(('prompt', 'roll')), parts along dimension 0, may hold values from -8 to 8
- roll_kv: bfloat16 [256, 128, 256], P(('prompt', 'roll')), parts along dimension 0, may hold values from -8 to 8
- pre_grad: bfloat16 [16384, 1024], P(('prompt', 'roll')), parts along dimension 0, may hold values from -6 to 6
- roll_grad: bfloat16 [256, 128, 1024], P(('prompt', 'roll')), parts along dimension 0, may hold values from -6 to 6
- pre_len: int32 [16], P('prompt'), parts along dimension 0, may hold values from 512 to 1024, as said below
- roll_len: int32 [256], P(('prompt', 'roll')), parts along dimension 0, may hold values from 32 to 128, as said below
Outputs:
- pre_out: bfloat16 [16384, 1024], P(('prompt', 'roll')), parts along dimension 0
- roll_out: bfloat16 [256, 128, 1024], P(('prompt', 'roll')), parts along dimension 0
- pre_dq: bfloat16 [16384, 1024], P(('prompt', 'roll')), parts along dimension 0
- roll_dq: bfloat16 [256, 128, 1024], P(('prompt', 'roll')), parts along dimension 0
- pre_dkv: bfloat16 [16384, 256], P(('prompt', 'roll')), parts along dimension 0
- roll_dkv: bfloat16 [256, 128, 256], P(('prompt', 'roll')), parts along dimension 0
There are 16 independent parts, one for each index of `prompt`. A program takes and returns all parts, laid end to end along the dimension named above; each array names one. Nothing has to cross between parts.
Inputs may be any that keep to these rules, and one draw needn't show every extreme that they name: `pre_len`: valid prefix positions of the prompt; later positions are padding. `roll_len`: valid tokens of each rollout; later tokens are padding; one rollout of each prompt has 128.
All inputs are finite; a program needn't handle non-finite values.
Results may differ from a plain program's by a relative error of at most 0.03.
Values may be sent and summed in bfloat16 or wider, within the bound.
A program may use at most 64 MiB of HBM per device.

v0:
```python
import jax
import jax.numpy as jnp
from jax import lax
from jax.sharding import PartitionSpec as P

masked_score = -1e30


def empty_state(head_count, row_count, head_dim):
    return (
        jnp.full((head_count, row_count), masked_score, jnp.float32),
        jnp.zeros((head_count, row_count), jnp.float32),
        jnp.zeros((head_count, row_count, head_dim), jnp.float32),
    )


def fold_step(partial_value, query, key_rows, val_rows, allowed, score_scale):
    row_max, row_sum, weighted = partial_value
    logits = (
        jnp.einsum("rhd,kd->hrk", query, key_rows, preferred_element_type=jnp.float32) * score_scale
    )
    new_max = jnp.maximum(row_max, jnp.max(jnp.where(allowed[None], logits, masked_score), axis=-1))
    factor = jnp.exp(row_max - new_max)
    expo = jnp.where(allowed[None], jnp.exp(logits - new_max[..., None]), 0.0)
    row_sum = row_sum * factor + jnp.sum(expo, axis=-1)
    weighted = weighted * factor[..., None] + jnp.einsum(
        "hrk,kd->hrd", expo.astype(jnp.bfloat16), val_rows, preferred_element_type=jnp.float32
    )
    return (new_max, row_sum, weighted)


def finish(partial_value, live_rows, grads):
    row_max, row_sum, weighted = partial_value
    output = (weighted / row_sum[..., None]).transpose(1, 0, 2)
    output = jnp.where(live_rows[:, None, None], output, 0.0).astype(jnp.bfloat16)
    log_total = row_max + jnp.log(row_sum)
    row_dot = jnp.sum(grads.astype(jnp.float32) * output.astype(jnp.float32), axis=-1).T
    return (output, log_total, row_dot)


def back_step(query, grads, key_rows, val_rows, allowed, log_total, row_dot, score_scale):
    logits = (
        jnp.einsum("rhd,kd->hrk", query, key_rows, preferred_element_type=jnp.float32) * score_scale
    )
    probs = jnp.where(allowed[None], jnp.exp(logits - log_total[..., None]), 0.0)
    grad_probs = jnp.einsum("rhd,kd->hrk", grads, val_rows, preferred_element_type=jnp.float32)
    grad_logits = (probs * (grad_probs - row_dot[..., None])).astype(jnp.bfloat16)
    grad_vals = jnp.einsum(
        "hrk,rhd->kd", probs.astype(jnp.bfloat16), grads, preferred_element_type=jnp.float32
    )
    grad_keys = (
        jnp.einsum("hrk,rhd->kd", grad_logits, query, preferred_element_type=jnp.float32)
        * score_scale
    )
    grad_query = (
        jnp.einsum("hrk,kd->rhd", grad_logits, key_rows, preferred_element_type=jnp.float32)
        * score_scale
    )
    return (grad_query, grad_keys, grad_vals)


def on_device(pre_q, pre_kv, roll_q, roll_kv, pre_grad, roll_grad, pre_len, roll_len):
    group_size = lax.axis_size("roll")
    device_index = lax.axis_index("roll")
    head_dim = pre_kv.shape[1] // 2
    row_width = pre_q.shape[1]
    head_count = row_width // head_dim
    shard_rows = pre_q.shape[0]
    resp_rows = roll_q.shape[1]
    score_scale = head_dim ** (-0.5)
    prefix_len = pre_len[0]
    resp_len = roll_len[0]
    local_rows = jnp.arange(shard_rows, dtype=jnp.int32)
    query_pos = device_index * shard_rows + local_rows
    group_count = 1
    group_rows = shard_rows // group_count
    pre_live = query_pos < prefix_len
    pre_query = pre_q.reshape(shard_rows, head_count, head_dim)
    pre_grads = jnp.where(
        pre_live[:, None, None],
        pre_grad.reshape(shard_rows, head_count, head_dim),
        jnp.zeros((), jnp.bfloat16),
    )
    resp_pos = jnp.arange(resp_rows, dtype=jnp.int32)
    roll_live = resp_pos < resp_len
    roll_query = roll_q[0].reshape(resp_rows, head_count, head_dim)
    roll_grads = jnp.where(
        roll_live[:, None, None],
        roll_grad[0].reshape(resp_rows, head_count, head_dim),
        jnp.zeros((), jnp.bfloat16),
    )
    group_last = [jnp.max(query_pos)]

    def masks(count):
        key_pos = jnp.arange(count, dtype=jnp.int32)
        roll_ok = jnp.broadcast_to((key_pos < prefix_len)[None, :], (resp_rows, count))
        pre_ok = (key_pos[None, :] <= query_pos[:, None]) & (key_pos < prefix_len)[None, :]
        return (roll_ok, pre_ok)

    initial = (
        empty_state(head_count, resp_rows, head_dim),
        tuple((empty_state(head_count, group_rows, head_dim) for part_index in range(group_count))),
    )
    block_kv = lax.all_gather(pre_kv, "roll", axis=0, tiled=True)
    key_rows = block_kv[:, :head_dim]
    val_rows = block_kv[:, head_dim:]
    roll_ok, pre_ok = masks(block_kv.shape[0])
    roll_state = fold_step(initial[0], roll_query, key_rows, val_rows, roll_ok, score_scale)
    lower = 0
    part_query = pre_query
    part_ok = pre_ok

    def advance_part(partial_value, part_query=part_query, part_ok=part_ok):
        return fold_step(partial_value, part_query, key_rows, val_rows, part_ok, score_scale)

    states = [
        lax.cond(
            jnp.int32(0) <= group_last[0],
            advance_part,
            lambda partial_value: partial_value,
            initial[1][0],
        )
    ]
    roll_state, part_states = (roll_state, tuple(states))
    pre_state = tuple(
        (jnp.concatenate([state[field] for state in part_states], axis=1) for field in range(3))
    )
    roll_keys = roll_kv[0, :, :head_dim]
    roll_vals = roll_kv[0, :, head_dim:]
    own_ok = (resp_pos[None, :] <= resp_pos[:, None]) & (resp_pos < resp_len)[None, :]
    roll_state = fold_step(roll_state, roll_query, roll_keys, roll_vals, own_ok, score_scale)
    roll_output, roll_total, roll_dot = finish(roll_state, roll_live, roll_grads)
    pre_output, pre_total, pre_dot = finish(pre_state, pre_live, pre_grads)
    own_dq, own_dk, own_dv = back_step(
        roll_query, roll_grads, roll_keys, roll_vals, own_ok, roll_total, roll_dot, score_scale
    )
    back_init = (
        own_dq,
        tuple(
            (
                jnp.zeros((group_rows, head_count, head_dim), jnp.float32)
                for part_index in range(group_count)
            )
        ),
        jnp.zeros((group_size * shard_rows, 2 * head_dim), jnp.float32),
    )
    block_kv = lax.all_gather(pre_kv, "roll", axis=0, tiled=True)
    backward_key_rows = block_kv[:, :head_dim]
    backward_val_rows = block_kv[:, head_dim:]
    roll_ok, pre_ok = masks(block_kv.shape[0])
    grad_query, grad_keys, grad_vals = back_step(
        roll_query,
        roll_grads,
        backward_key_rows,
        backward_val_rows,
        roll_ok,
        roll_total,
        roll_dot,
        score_scale,
    )
    part_index = 0
    lower = part_index * group_rows
    upper = lower + group_rows

    def prefix_part(summed, lower=lower, upper=upper):
        more_query, more_keys, more_vals = back_step(
            pre_query,
            pre_grads,
            backward_key_rows,
            backward_val_rows,
            pre_ok,
            pre_total,
            pre_dot,
            score_scale,
        )
        return (more_query, more_keys, more_vals)

    def skipped(summed):
        return (summed, jnp.zeros_like(grad_keys), jnp.zeros_like(grad_vals))

    part_sum, more_keys, more_vals = lax.cond(
        jnp.int32(0) <= group_last[part_index], prefix_part, skipped, back_init[1][part_index]
    )
    sums = [part_sum]
    grad_keys = grad_keys + more_keys
    grad_vals = grad_vals + more_vals
    key_grads = jnp.concatenate([grad_keys, grad_vals], axis=1)
    grad_buffer = key_grads
    roll_dq_sum, part_sums, grad_buffer = (back_init[0] + grad_query, tuple(sums), grad_buffer)
    pre_dq_sum = jnp.concatenate(list(part_sums), axis=0)
    pre_dkv = lax.psum_scatter(
        grad_buffer.astype(jnp.bfloat16), "roll", scatter_dimension=0, tiled=True
    )
    roll_dkv = jnp.concatenate([own_dk, own_dv], axis=1).astype(jnp.bfloat16)[None]
    roll_out = roll_output.reshape(resp_rows, row_width)[None]
    roll_dq = roll_dq_sum.astype(jnp.bfloat16).reshape(resp_rows, row_width)[None]
    pre_out = pre_output.reshape(shard_rows, row_width)
    pre_dq = pre_dq_sum.astype(jnp.bfloat16).reshape(shard_rows, row_width)
    return (pre_out, roll_out, pre_dq, roll_dq, pre_dkv, roll_dkv)


def solution(mesh):
    in_specs = (
        P(("prompt", "roll"), None),
        P(("prompt", "roll"), None),
        P(("prompt", "roll"), None, None),
        P(("prompt", "roll"), None, None),
        P(("prompt", "roll"), None),
        P(("prompt", "roll"), None, None),
        P("prompt"),
        P(("prompt", "roll")),
    )
    out_specs = (
        P(("prompt", "roll"), None),
        P(("prompt", "roll"), None, None),
        P(("prompt", "roll"), None),
        P(("prompt", "roll"), None, None),
        P(("prompt", "roll"), None),
        P(("prompt", "roll"), None, None),
    )
    return jax.shard_map(
        on_device, mesh=mesh, in_specs=in_specs, out_specs=out_specs, check_vma=False
    )
```

profile of v0, /device:TPU:1, one launch (start us, length us, event | category | flops | bytes accessed | tf_op | source)
XLA Modules:
  0.0 151.2 jit_solution(2351324646143192350)
XLA Ops:
  7.2 0.6 fusion.127
  9.3 1.1 copy.140
  10.4 36.2 %all_gather.4 = bf16[1024,256]{1,0:T(8,128)(2,1)S(1)} all-gather(bf16[64,256]{1,0:T(8,128)(2,1)} %param.13), channel_id=1, replica_groups=mesh['prompt'=16,'roll'=16] {'roll'}, dimensions={0}, use_global_device_ids=true | all-gather | bytes 557056 | tf_op jit(solution)/shard_map/all_gather | solution.py:104
  46.7 0.7 fusion.33
  47.5 0.2 select_reduce_fusion
  47.9 0.6 copy-done.15
  48.5 0.9 fusion.39
  49.5 0.6 log_add_fusion
  50.1 0.6 bitcast_add_fusion
  51.4 0.1 fusion.99
  51.6 0.8 copy.93
  52.4 4.6 %conditional.2 = (f32[8,64]{1,0:T(8,128)}, f32[8,64]{1,0:T(8,128)S(1)}, f32[8,64]{1,0:T(8,128)S(1)}, f32[8,64,128]{2,0,1:T(8,128)S(1)}) conditional(s32[]{:T(128)} %convert_element_type.76, () %tuple.28, (pred[64,1024]{1,0:T(8,128)(4,1)S(1)}, bf16[1024,128]{1,0:T(8,128)(2,1)S(1)}, bf16[64,8,128]{2,1,0:T(8,128)(2,1)S(1)}, ...), branch_computations={%region_1.2_spmd, %region_2.5_spmd} | conditional | flops 274270208 | bytes 7954464 | solution.py:117
  52.4 0.6 fusion
  53.0 0.6 exponential_multiply_fusion
  53.6 1.2 convolution_add_fusion
  54.9 1.3 fusion.4
  56.2 0.2 copy.134
  56.4 0.7 fusion.133
  57.1 0.4 multiply_reduce_fusion.1
  57.6 5.8 %conditional.3 = (bf16[64,1024]{1,0:T(8,128)(2,1)}, f32[1024,128]{0,1:T(8,128)S(1)}, f32[1024,128]{0,1:T(8,128)S(1)}) conditional(s32[]{:T(128)} %convert_element_type.76, () %tuple.30, (pred[64,1024]{1,0:T(8,128)(4,1)S(1)}, bf16[1024,128]{1,0:T(8,128)(2,1)S(1)}, bf16[64,8,128]{2,1,0:T(8,128)(2,1)S(1)}, f32[8,64]{1,0:T(8,128)}, ...), branch_computations={%region_10.11_spmd, %region_11.12_spmd} | conditional | flops 675021312 | bytes 13318168 | solution.py:181
  57.6 0.7 add.64
  58.3 0.6 fusion.19
  59.0 0.3 convolution_bitcast_fusion
  59.3 0.4 fusion.17
  59.8 0.4 fusion.22
  60.2 1.3 fusion.20
  61.5 1.2 copy.136
  62.7 0.7 copy.162
  63.5 3.3 %fusion.68 = f32[128,8,128]{0,2,1:T(8,128)S(1)} fusion(f32[1024,128,8]{1,0,2:T(8,128)} %copy-done, f32[8,128]{1,0:T(8,128)S(1)} %copy-done.18, pred[1024]{0:T(1024)(128)(4,1)S(1)} %copy-done.20, f32[128,8]{0,1:T(8,128)S(1)} %copy-done.25, f32[128,8]{0,1:T(8,128)S(1)} %copy-done.26, bf16[1024,256]{1,0:T(8,128)(2,1)S(1)} %all_gather.4), kind=kOutput, calls=%fused_computation.77 | convolution fusion | flops 272891904 | bytes 4994048 | tf_op jit(solution)/shard_map/hrk,kd->hrd/dot_general | solution.py:26
  66.8 0.3 copy-done.1
  67.1 1.0 fusion.71
  68.2 1.0 multiply_reduce_fusion
  69.2 1.6 %fusion.32 = bf16[8,128,1024]{1,2,0:T(8,128)(2,1)S(1)} fusion(f32[1024,128,8]{1,0,2:T(8,128)S(1)} %copy-done.1, f32[8,128]{1,0:T(8,128)S(1)} %bitcast.271, f32[8,128]{1,0:T(8,128)S(1)} %copy-done.22, pred[1024]{0:T(1024)(128)(4,1)S(1)} %copy-done.21, bf16[128,8,128]{0,2,1:T(8,128)(2,1)S(1)} %bitcast.264, pred[128]{0:T(512)(128)(4,1)S(1)} %copy-done.28, ...), kind=kOutput, calls=%fused_computation.43 | convolution fusion | flops 274857984 | bytes 6825472 | tf_op jit(solution)/shard_map/rhd,kd->hrk/dot_general | solution.py:46
  70.8 0.8 fusion.77
  71.7 0.8 pad_maximum_fusion
  72.5 2.1 %copy.131 = bf16[1024,256]{1,0:T(8,128)(2,1)} copy(bf16[1024,256]{0,1:T(8,128)(2,1)} %pad_maximum_fusion) | data formatting | bytes 1048576
  74.6 1.1 select_bitcast_fusion
  75.7 1.2 fusion.82
  76.9 0.7 copy.163
  77.6 0.2 fusion.76
  77.9 0.2 fusion.81
  78.1 0.4 copy-done.5
  78.6 0.7 copy.111
  79.3 0.5 fusion.90
  79.8 0.3 fusion.75
  80.1 0.9 copy.109
  81.0 0.8 copy.108
  81.8 62.5 %reduce-scatter.4.cloned.1.call-done = bf16[64,256]{1,0:T(8,128)(2,1)} async-done(((bf16[1024,256]{1,0:T(8,128)(2,1)}), bf16[64,256]{1,0:T(8,128)(2,1)}) %reduce-scatter.4.cloned.1.call-update) | async-done | bytes 32784
  (75 shorter events, 0.9 us)
Async XLA Ops:
  7.2 137.2 %reduce-scatter.4.cloned.1.call-start = ((), (), s32[]{:S(2)}) async-start(), calls=%async_computation.1 | async-start | bytes 557056
  9.2 38.3 %copy-start.27 = (pred[128]{0:T(512)(128)(4,1)}, pred[128]{0:T(512)(128)(4,1)S(1)}, u32[]{:S(2)}) copy-start(pred[128]{0:T(512)(128)(4,1)S(1)} %iota_compare_fusion.3) | copy-start | bytes 388
  9.2 42.2 %copy-start.19 = (pred[1024]{0:T(1024)(128)(4,1)}, pred[1024]{0:T(1024)(128)(4,1)S(1)}, u32[]{:S(2)}) copy-start(pred[1024]{0:T(1024)(128)(4,1)S(1)} %iota_compare_fusion.2) | copy-start | bytes 3076
  46.7 0.8 copy-start.11
  47.5 2.0 %copy-start = (f32[1024,128,8]{1,0,2:T(8,128)}, f32[1024,128,8]{1,0,2:T(8,128)S(1)}, u32[]{:S(2)}) copy-start(f32[1024,128,8]{1,0,2:T(8,128)S(1)} %get-tuple-element.123) | copy-start | bytes 12582916
  47.8 0.7 copy-start.15
  47.8 1.7 %copy-start.17 = (f32[8,128]{1,0:T(8,128)}, f32[8,128]{1,0:T(8,128)S(1)}, u32[]{:S(2)}) copy-start(f32[8,128]{1,0:T(8,128)S(1)} %get-tuple-element.119) | copy-start | bytes 12292
  48.5 3.0 %copy-start.9 = (bf16[64,1024]{1,0:T(8,128)(2,1)S(1)}, bf16[64,1024]{1,0:T(8,128)(2,1)}, u32[]{:S(2)}) copy-start(bf16[64,1024]{1,0:T(8,128)(2,1)} %param.12) | copy-start | bytes 393220
  48.5 3.0 %copy-start.10 = (bf16[64,1024]{1,0:T(8,128)(2,1)S(1)}, bf16[64,1024]{1,0:T(8,128)(2,1)}, u32[]{:S(2)}) copy-start(bf16[64,1024]{1,0:T(8,128)(2,1)} %param.16) | copy-start | bytes 393220
  48.5 3.1 %copy-start.4 = (bf16[1,128,1024]{2,1,0:T(8,128)(2,1)S(1)}, bf16[1,128,1024]{2,1,0:T(8,128)(2,1)}, u32[]{:S(2)}) copy-start(bf16[1,128,1024]{2,1,0:T(8,128)(2,1)} %param.17) | copy-start | bytes 786436
  57.5 5.9 %copy-start.18 = (f32[8,128]{1,0:T(8,128)S(1)}, f32[8,128]{1,0:T(8,128)}, u32[]{:S(2)}) copy-start(f32[8,128]{1,0:T(8,128)} %copy-done.17) | copy-start | bytes 12292
  57.5 5.9 %copy-start.20 = (pred[1024]{0:T(1024)(128)(4,1)S(1)}, pred[1024]{0:T(1024)(128)(4,1)}, u32[]{:S(2)}) copy-start(pred[1024]{0:T(1024)(128)(4,1)} %copy-done.19) | copy-start | bytes 3076
  57.5 5.9 %copy-start.25 = (f32[128,8]{0,1:T(8,128)S(1)}, f32[128,8]{0,1:T(8,128)}, u32[]{:S(2)}) copy-start(f32[128,8]{0,1:T(8,128)} %get-tuple-element.116) | copy-start | bytes 12292
  57.5 5.9 %copy-start.26 = (f32[128,8]{0,1:T(8,128)S(1)}, f32[128,8]{0,1:T(8,128)}, u32[]{:S(2)}) copy-start(f32[128,8]{0,1:T(8,128)} %get-tuple-element.117) | copy-start | bytes 12292
  63.4 3.4 %copy-start.2 = (f32[1024,128]{0,1:T(8,128)}, f32[1024,128]{0,1:T(8,128)S(1)}, u32[]{:S(2)}) copy-start(f32[1024,128]{0,1:T(8,128)S(1)} %get-tuple-element.102) | copy-start | bytes 1572868
  63.4 3.6 %copy-start.1 = (f32[1024,128,8]{1,0,2:T(8,128)S(1)}, f32[1024,128,8]{1,0,2:T(8,128)}, u32[]{:S(2)}) copy-start(f32[1024,128,8]{1,0,2:T(8,128)} %copy-done) | copy-start | bytes 12582916
  63.4 3.6 %copy-start.7 = (bf16[1,128,1024]{1,2,0:T(8,128)(2,1)S(1)}, bf16[1,128,1024]{1,2,0:T(8,128)(2,1)}, u32[]{:S(2)}) copy-start(bf16[1,128,1024]{1,2,0:T(8,128)(2,1)} %copy.93) | copy-start | bytes 786436
  63.5 3.6 %copy-start.22 = (f32[8,128]{1,0:T(8,128)S(1)}, f32[8,128]{1,0:T(8,128)}, u32[]{:S(2)}) copy-start(f32[8,128]{1,0:T(8,128)} %log_add_fusion) | copy-start | bytes 12292
  63.5 3.6 %copy-start.28 = (pred[128]{0:T(512)(128)(4,1)S(1)}, pred[128]{0:T(512)(128)(4,1)}, u32[]{:S(2)}) copy-start(pred[128]{0:T(512)(128)(4,1)} %copy-done.27) | copy-start | bytes 388
  67.1 1.1 copy-start.12
  67.1 1.1 copy-start.16
  67.1 1.1 copy-start.24
  68.1 1.1 copy-start.21
  69.2 1.6 %copy-start.29 = (f32[128,8]{0,1:T(8,128)}, f32[128,8]{0,1:T(8,128)S(1)}, u32[]{:S(2)}) copy-start(f32[128,8]{0,1:T(8,128)S(1)} %get-tuple-element.124) | copy-start | bytes 12292
  69.2 1.6 %copy-start.3 = (f32[1024,128]{0,1:T(8,128)S(1)}, f32[1024,128]{0,1:T(8,128)}, u32[]{:S(2)}) copy-start(f32[1024,128]{0,1:T(8,128)} %copy-done.2) | copy-start | bytes 1572868
  74.6 3.0 %copy-start.13 = (bf16[1,128,256]{2,1,0:T(8,128)(2,1)S(1)}, bf16[1,128,256]{2,1,0:T(8,128)(2,1)}, u32[]{:S(2)}) copy-start(bf16[1,128,256]{2,1,0:T(8,128)(2,1)} %param.15) | copy-start | bytes 196612
  74.6 3.0 %copy-start.23 = (f32[8,128]{1,0:T(8,128)S(1)}, f32[8,128]{1,0:T(8,128)}, u32[]{:S(2)}) copy-start(f32[8,128]{1,0:T(8,128)} %log_add_fusion) | copy-start | bytes 12292
  74.6 3.0 %copy-start.30 = (f32[128,8]{0,1:T(8,128)S(1)}, f32[128,8]{0,1:T(8,128)}, u32[]{:S(2)}) copy-start(f32[128,8]{0,1:T(8,128)} %copy-done.29) | copy-start | bytes 12292
  77.9 0.7 copy-start.5
  77.9 1.9 %copy-start.14 = (bf16[1,128,256]{2,1,0:T(8,128)(2,1)S(1)}, bf16[1,128,256]{2,1,0:T(8,128)(2,1)}, u32[]{:S(2)}) copy-start(bf16[1,128,256]{2,1,0:T(8,128)(2,1)} %param.15) | copy-start | bytes 196612
  78.6 1.3 copy-start.6
  79.3 1.6 %copy-start.8 = (bf16[128,8,128]{0,2,1:T(8,128)(2,1)S(1)}, bf16[128,8,128]{0,2,1:T(8,128)(2,1)}, u32[]{:S(2)}) copy-start(bf16[128,8,128]{0,2,1:T(8,128)(2,1)} %get-tuple-element.125) | copy-start | bytes 786436
Sparse Core Ops, SparseCore 0:
  74.7 69.5 reduce-scatter.3
where the time goes:
time: 153 us; the launch traced here: 151 us
  waiting for transfers between devices  62.5 us (41%)
  blocking collectives  36.2 us (24%)
  between operations  16.5 us (11%)
  matrix products  16.1 us (11%)
  local copies, waits for them, and re-layouts  11.1 us (7%)
  other arithmetic  8.63 us (6%)
    unnamed x2, waiting for transfers between devices  62.5 us
    all_gather x1, blocking collectives, on_device(): block_kv = lax.all_gather(pre_kv, 'roll', axis=0, tiled=True)  36.2 us
    unnamed x71, local copies, waits for them, and re-layouts  7.75 us
    dot_general x3, matrix products, fold_step(): jnp.einsum('hrk,kd->hrd', expo.astype(jnp.bfloat16), val_rows, preferred_...  5.56 us
  transfers between devices with their start and end apart: 1, of which 1 were waited for; matrix products, arithmetic and copies ran while one was open for 4% of the time, Pallas kernels for 0%

commit v1 on v0

v1 whole, which is shorter than its diff:
```python
import functools

import jax
import jax.numpy as jnp
from jax import lax
from jax.experimental import pallas as pl
from jax.experimental.pallas import tpu as pltpu
from jax.sharding import PartitionSpec as P

F32 = jnp.float32
BF16 = jnp.bfloat16
MESH = pl.DeviceIdType.MESH
masked_score = -1e30
HALVES, ROW, CORES = 2, 4, 2
BLOCK = 64
RESP = 128
HEADS = 8
HD = 128
GROUP = HALVES * ROW * CORES
CHUNK = ROW * BLOCK
PREFIX = GROUP * BLOCK
ROLL_ROWS = HEADS * RESP
ROWS = HEADS * (RESP + BLOCK)
SCALE = HD**-0.5
LOG2E = 1.4426950408889634


def dot(left, right, left_dim, right_dim):
    return lax.dot_general(
        left, right, (((left_dim,), (right_dim,)), ((), ())), preferred_element_type=F32
    )


def slot(half, core, place):
    return (half * CORES + core) * ROW + place


def block_of(half, core, place):
    return pl.ds(slot(half, core, place) * BLOCK, BLOCK)


def chunk_of(half, core):
    return pl.ds((half * CORES + core) * CHUNK, CHUNK)


def fold8(values, combine):
    return combine(values.reshape(values.shape[0] // 8, 8, values.shape[1]), axis=0)


def kernel(
    pre_len_ref,
    roll_len_ref,
    pre_q,
    pre_kv,
    roll_q,
    roll_kv,
    pre_grad,
    roll_grad,
    pre_out,
    roll_out,
    pre_dq,
    roll_dq,
    pre_dkv,
    roll_dkv,
    rq,
    rg,
    pq,
    pg,
    rkv,
    kvs,
    queries,
    grads,
    score,
    weight,
    gradp,
    keys_t,
    vals_t,
    to_core,
    from_core,
    own_sum,
    to_row,
    from_row,
    to_half,
    from_half,
    load_sem,
    send_sem,
    recv_sem,
    sum_send_sem,
    sum_recv_sem,
):
    me = lax.axis_index("roll")
    my_half, my_place, my_core = me // (ROW * CORES), (me // CORES) % ROW, me % CORES

    def device(half, core, place):
        return (
            ((my_half + half) % HALVES) * (ROW * CORES)
            + ((my_place + place) % ROW) * CORES
            + (my_core + core) % CORES
        )

    partners = [(1, 0, 0), (0, 1, 0), (0, 0, 1), (0, 0, 3), (0, 0, 2)]
    barrier = pltpu.get_barrier_semaphore()
    for partner in partners:
        pl.semaphore_signal(
            barrier, inc=1, device_id={"roll": device(*partner)}, device_id_type=MESH
        )

    loads = []
    for index, (source, target) in enumerate(
        (
            (pre_kv, kvs.at[block_of(0, 0, 0)]),
            (roll_kv.at[0], rkv),
            (roll_q.at[0], rq),
            (pre_q, pq),
            (roll_grad.at[0], rg),
            (pre_grad, pg),
        )
    ):
        loads.append(pltpu.make_async_copy(source, target, load_sem.at[index]))
        loads[-1].start()

    def push(source, half, core, place, to):
        at = slot(half, core, place)
        copy = pltpu.make_async_remote_copy(
            src_ref=source,
            dst_ref=kvs.at[block_of(half, core, place)],
            send_sem=send_sem.at[at],
            recv_sem=recv_sem.at[at],
            device_id={"roll": device(*to)},
            device_id_type=MESH,
        )
        copy.start()
        return copy

    pl.semaphore_wait(barrier, len(partners))
    copies = {}
    copies[1, 0, 0] = push(pre_kv, 1, 0, 0, (1, 0, 0))
    for place in (1, 3, 2):
        copies[0, 0, ROW - place] = push(pre_kv, 0, 0, ROW - place, (0, 0, place))
    copies[0, 1, 0] = push(pre_kv, 0, 1, 0, (0, 1, 0))

    pre_len = pre_len_ref[0]
    roll_len = roll_len_ref[0]
    lane = lax.broadcasted_iota(jnp.int32, (1, ROWS), 1)
    is_roll = lane < ROLL_ROWS
    query_pos = me * BLOCK + lane % BLOCK
    limit = jnp.where(is_roll, pre_len - 1, jnp.minimum(query_pos, pre_len - 1))
    own_limit = jnp.minimum(lane[:, :ROLL_ROWS] % RESP, roll_len - 1)
    rows_left = jnp.where(is_roll, roll_len - lane % RESP, pre_len - query_pos)

    for load in loads:
        load.wait()
    roll_live = lax.broadcasted_iota(jnp.int32, (RESP, HD), 0) < roll_len
    pre_live = lax.broadcasted_iota(jnp.int32, (BLOCK, HD), 0) + me * BLOCK < pre_len
    none = jnp.zeros((), BF16)
    for head in range(HEADS):
        columns = slice(head * HD, (head + 1) * HD)
        at = pl.ds(head * RESP, RESP)
        queries[at, :] = rq[:, columns]
        grads[at, :] = jnp.where(roll_live, rg[:, columns], none)
        at = pl.ds(ROLL_ROWS + head * BLOCK, BLOCK)
        queries[at, :] = pq[:, columns]
        grads[at, :] = jnp.where(pre_live, pg[:, columns], none)

    own_rows = pl.ds(PREFIX, RESP)
    own_cols = slice(0, ROLL_ROWS)

    def transpose_in(half, core):
        at = chunk_of(half, core)
        keys_t[:, at] = kvs[at, 0:HD].T
        vals_t[:, at] = kvs[at, HD : 2 * HD].T

    def scores_of(half, core):
        at = chunk_of(half, core)
        row = lax.broadcasted_iota(jnp.int32, (CHUNK, 1), 0)
        owner = (
            ((my_half + half) % HALVES) * (ROW * CORES)
            + ((my_place + row // BLOCK) % ROW) * CORES
            + (my_core + core) % CORES
        )
        key_pos = owner * BLOCK + row % BLOCK
        logits = dot(kvs[at, 0:HD], queries[...], 1, 1) * (SCALE * LOG2E)
        logits = jnp.where(key_pos <= limit, logits, masked_score)
        score[at, :] = logits
        return fold8(logits, jnp.max)

    def widen(total, own, combine):
        return jnp.concatenate([combine(total[:, own_cols], own), total[:, ROLL_ROWS:]], axis=1)

    def expo_of(half, core, row_max):
        at = chunk_of(half, core)
        expo = jnp.exp2(score[at, :] - row_max)
        rounded = expo.astype(BF16)
        weight[at, :] = rounded
        return fold8(expo, jnp.sum), dot(vals_t[:, at], rounded, 1, 0)

    own_key = lax.broadcasted_iota(jnp.int32, (RESP, 1), 0)
    own_logits = dot(rkv[:, 0:HD], queries[own_cols, :], 1, 1) * (SCALE * LOG2E)
    own_logits = jnp.where(own_key <= own_limit, own_logits, masked_score)
    score[own_rows, own_cols] = own_logits
    own_max = fold8(own_logits, jnp.max)
    keys_t[:, own_rows] = rkv[:, 0:HD].T
    vals_t[:, own_rows] = rkv[:, HD : 2 * HD].T
    gradp[own_rows, own_cols] = dot(rkv[:, HD : 2 * HD], grads[own_cols, :], 1, 1)
    grad_t = grads[...].T.astype(F32)

    for place in (1, 3, 2):
        copies[0, 0, place].wait_recv()
        copies[0, 1, place] = push(
            kvs.at[block_of(0, 0, place)], 0, 1, place, (0, 1, 0)
        )
    transpose_in(0, 0)
    near_max = scores_of(0, 0)
    copies[1, 0, 0].wait_recv()
    for place in (1, 3, 2):
        copies[1, 0, ROW - place] = push(
            kvs.at[block_of(1, 0, 0)], 1, 0, ROW - place, (0, 0, place)
        )
    copies[1, 1, 0] = push(kvs.at[block_of(1, 0, 0)], 1, 1, 0, (0, 1, 0))
    for place in range(ROW):
        copies[0, 1, place].wait_recv()
    transpose_in(0, 1)
    near_max = jnp.maximum(near_max, scores_of(0, 1))
    near_max = widen(near_max, own_max, jnp.maximum)
    near_max = jnp.max(near_max, axis=0, keepdims=True)
    for place in (1, 3, 2):
        copies[1, 0, place].wait_recv()
        copies[1, 1, place] = push(
            kvs.at[block_of(1, 0, place)], 1, 1, place, (0, 1, 0)
        )
    near_sum, near_out = expo_of(0, 0, near_max)
    more_sum, more_out = expo_of(0, 1, near_max)
    near_sum, near_out = near_sum + more_sum, near_out + more_out
    expo = jnp.exp2(score[own_rows, own_cols] - near_max[:, own_cols])
    rounded = expo.astype(BF16)
    weight[own_rows, own_cols] = rounded
    near_sum = widen(near_sum, fold8(expo, jnp.sum), jnp.add)
    near_out = widen(near_out, dot(vals_t[:, own_rows], rounded, 1, 0), jnp.add)
    near_sum = jnp.sum(near_sum, axis=0, keepdims=True)
    for core in range(CORES):
        at = chunk_of(0, core)
        gradp[at, :] = dot(kvs[at, HD : 2 * HD], grads[...], 1, 1)

    transpose_in(1, 0)
    far_max = scores_of(1, 0)
    for place in range(ROW):
        copies[1, 1, place].wait_recv()
    transpose_in(1, 1)
    far_max = jnp.maximum(far_max, scores_of(1, 1))
    far_max = jnp.max(far_max, axis=0, keepdims=True)
    row_max = jnp.maximum(near_max, far_max)
    shrink = jnp.exp2(near_max - row_max)
    far_sum, far_out = expo_of(1, 0, row_max)
    more_sum, more_out = expo_of(1, 1, row_max)
    far_sum = jnp.sum(far_sum + more_sum, axis=0, keepdims=True)
    row_sum = near_sum * shrink + far_sum
    inverse = 1.0 / row_sum
    out_t = near_out * shrink + (far_out + more_out)
    out_t = (out_t * jnp.where(rows_left > 0, inverse, 0.0)).astype(BF16)
    row_dot = jnp.sum(grad_t * out_t.astype(F32), axis=0, keepdims=True)
    factors = (shrink * inverse, inverse)

    def back(at, cols, grad_probs, factor):
        probs = weight[at, cols].astype(F32) * factor[:, cols]
        grad_logits = (probs * (grad_probs - row_dot[:, cols])).astype(BF16)
        weight[at, cols] = grad_logits
        grad_vals = dot(probs.astype(BF16), grads[cols, :], 1, 0)
        grad_keys = dot(grad_logits, queries[cols, :], 1, 0) * SCALE
        return grad_keys, grad_vals

    def prefix_back(half, core):
        at = chunk_of(half, core)
        if half == 0:
            grad_probs = gradp[at, :]
        else:
            grad_probs = dot(kvs[at, HD : 2 * HD], grads[...], 1, 1)
        return back(at, slice(0, ROWS), grad_probs, factors[half])

    def ship(source, target, index, to):
        copy = pltpu.make_async_remote_copy(
            src_ref=source,
            dst_ref=target,
            send_sem=sum_send_sem.at[index],
            recv_sem=sum_recv_sem.at[index],
            device_id={"roll": device(*to)},
            device_id_type=MESH,
        )
        copy.start()
        return copy

    sums = {}

    def send_core(half):
        grad_keys, grad_vals = prefix_back(half, 1)
        to_core[half, :, 0:HD] = grad_keys.astype(BF16)
        to_core[half, :, HD : 2 * HD] = grad_vals.astype(BF16)
        sums["core", half] = ship(to_core.at[half], from_core.at[half], half, (0, 1, 0))

    def send_row(half):
        grad_keys, grad_vals = prefix_back(half, 0)
        own_sum[half, :, 0:HD] = grad_keys
        own_sum[half, :, HD : 2 * HD] = grad_vals
        sums["core", half].wait_recv()
        for place in (2, 1, 3):
            at = pl.ds(place * BLOCK, BLOCK)
            total = own_sum[half, at, :] + from_core[half, at, :].astype(F32)
            to_row[half, place] = total.astype(BF16)
            sums["row", half, place] = ship(
                to_row.at[half, place],
                from_row.at[half, place],
                CORES + half * ROW + place,
                (0, 0, place),
            )

    def row_total(half):
        at = pl.ds(0, BLOCK)
        total = own_sum[half, at, :] + from_core[half, at, :].astype(F32)
        for place in (1, 3, 2):
            sums["row", half, place].wait_recv()
            total = total + from_row[half, place].astype(F32)
        return total

    send_core(1)
    send_row(1)
    send_core(0)
    to_half[...] = row_total(1).astype(BF16)
    sums["half"] = ship(to_half, from_half, CORES + HALVES * ROW, (1, 0, 0))
    send_row(0)

    grad_keys, grad_vals = back(
        own_rows, own_cols, gradp[own_rows, own_cols], factors[0]
    )
    roll_dkv[0, :, 0:HD] = grad_keys.astype(BF16)
    roll_dkv[0, :, HD : 2 * HD] = grad_vals.astype(BF16)
    out = out_t.T
    for head in range(HEADS):
        columns = slice(head * HD, (head + 1) * HD)
        roll_out[0, :, columns] = out[head * RESP : (head + 1) * RESP]
        at = ROLL_ROWS + head * BLOCK
        pre_out[:, columns] = out[at : at + BLOCK]
    grad_query = dot(keys_t[:, 0:PREFIX], weight[0:PREFIX, :], 1, 0)
    grad_query = widen(
        grad_query, dot(keys_t[:, own_rows], weight[own_rows, own_cols], 1, 0), jnp.add
    )
    grad_query = (grad_query * SCALE).astype(BF16).T
    for head in range(HEADS):
        columns = slice(head * HD, (head + 1) * HD)
        roll_dq[0, :, columns] = grad_query[head * RESP : (head + 1) * RESP]
        at = ROLL_ROWS + head * BLOCK
        pre_dq[:, columns] = grad_query[at : at + BLOCK]

    total = row_total(0)
    sums["half"].wait_recv()
    pre_dkv[...] = (total + from_half[...].astype(F32)).astype(BF16)
    for copy in (*copies.values(), *sums.values()):
        copy.wait_send()


def on_device(pre_q, pre_kv, roll_q, roll_kv, pre_grad, roll_grad, pre_len, roll_len):
    smem = pl.BlockSpec(memory_space=pltpu.SMEM)
    vmem = pl.BlockSpec(memory_space=pltpu.VMEM)
    anywhere = pl.BlockSpec(memory_space=pl.ANY)
    like = lambda array: jax.ShapeDtypeStruct(array.shape, BF16)
    copies = GROUP
    sums = CORES + HALVES * ROW + 1
    return pl.pallas_call(
        kernel,
        out_shape=(
            like(pre_q),
            like(roll_q),
            like(pre_q),
            like(roll_q),
            like(pre_kv),
            like(roll_kv),
        ),
        in_specs=[smem] * 2 + [anywhere] * 6,
        out_specs=[vmem] * 6,
        scratch_shapes=[
            pltpu.VMEM((RESP, HEADS * HD), BF16),
            pltpu.VMEM((RESP, HEADS * HD), BF16),
            pltpu.VMEM((BLOCK, HEADS * HD), BF16),
            pltpu.VMEM((BLOCK, HEADS * HD), BF16),
            pltpu.VMEM((RESP, 2 * HD), BF16),
            pltpu.VMEM((PREFIX, 2 * HD), BF16),
            pltpu.VMEM((ROWS, HD), BF16),
            pltpu.VMEM((ROWS, HD), BF16),
            pltpu.VMEM((PREFIX + RESP, ROWS), F32),
            pltpu.VMEM((PREFIX + RESP, ROWS), BF16),
            pltpu.VMEM((PREFIX + RESP, ROWS), F32),
            pltpu.VMEM((HD, PREFIX + RESP), BF16),
            pltpu.VMEM((HD, PREFIX + RESP), BF16),
            pltpu.VMEM((HALVES, CHUNK, 2 * HD), BF16),
            pltpu.VMEM((HALVES, CHUNK, 2 * HD), BF16),
            pltpu.VMEM((HALVES, CHUNK, 2 * HD), F32),
            pltpu.VMEM((HALVES, ROW, BLOCK, 2 * HD), BF16),
            pltpu.VMEM((HALVES, ROW, BLOCK, 2 * HD), BF16),
            pltpu.VMEM((BLOCK, 2 * HD), BF16),
            pltpu.VMEM((BLOCK, 2 * HD), BF16),
            pltpu.SemaphoreType.DMA((6,)),
            pltpu.SemaphoreType.DMA((copies,)),
            pltpu.SemaphoreType.DMA((copies,)),
            pltpu.SemaphoreType.DMA((sums,)),
            pltpu.SemaphoreType.DMA((sums,)),
        ],
        compiler_params=pltpu.CompilerParams(
            collective_id=0, has_side_effects=True, vmem_limit_bytes=56 << 20
        ),
    )(pre_len, roll_len, pre_q, pre_kv, roll_q, roll_kv, pre_grad, roll_grad)


def solution(mesh):
    in_specs = (
        P(("prompt", "roll"), None),
        P(("prompt", "roll"), None),
        P(("prompt", "roll"), None, None),
        P(("prompt", "roll"), None, None),
        P(("prompt", "roll"), None),
        P(("prompt", "roll"), None, None),
        P("prompt"),
        P(("prompt", "roll")),
    )
    out_specs = (
        P(("prompt", "roll"), None),
        P(("prompt", "roll"), None, None),
        P(("prompt", "roll"), None),
        P(("prompt", "roll"), None, None),
        P(("prompt", "roll"), None),
        P(("prompt", "roll"), None, None),
    )
    return jax.shard_map(
        on_device, mesh=mesh, in_specs=in_specs, out_specs=out_specs, check_vma=False
    )
```

time: 153 us -> 40.4 us (0.26)
  waiting for transfers between devices: 62.5 us -> 0 us
  blocking collectives: 36.2 us -> 0 us
  Pallas kernels: 0 us -> 32.3 us
  matrix products: 16.1 us -> 0 us
  between operations: 16.5 us -> 1.95 us
  other arithmetic: 8.63 us -> 0 us
  local copies, waits for them, and re-layouts: 11.1 us -> 5.84 us
    unnamed x2 -> x0, waiting for transfers between devices: 62.5 us -> none
    all_gather x1 -> x0, blocking collectives: 36.2 us -> none  [on_device(): block_kv = lax.all_gather(pre_kv, 'roll', axis=0, tiled=True)]
    pallas_call x0 -> x1, Pallas kernels: none -> 32.3 us  [on_device(): pl.pallas_call(kernel, out_shape=(like(pre_q), like(roll_q), like(pre_q),...]
    dot_general x19 -> x0, matrix products: 16.1 us -> none  [the longest x3 5.56 us: fold_step(): jnp.einsum('hrk,kd->hrd', expo.astype(jnp.bfloat16), val_rows, preferred_...]
    reduce_sum x4 -> x0, other arithmetic: 2.65 us -> none  [the longest x3 2.29 us: fold_step(): row_sum = row_sum * factor + jnp.sum(expo, axis=-1)]
    add x4 -> x0, other arithmetic: 1.92 us -> none  [the longest x2 1.31 us: finish(): log_total = row_max + jnp.log(row_sum)]
    unnamed x71 -> x16, local copies, waits for them, and re-layouts: 7.75 us -> 5.84 us
  transfers between devices with their start and end apart: 1 -> 0, of which waited for: 1 -> 0; matrix products, arithmetic and copies ran while one was open for 4% -> 0% of each run, Pallas kernels for 0% -> 0%
where the time goes in v1:
time: 40.4 us; the launch traced here: 40.1 us
  Pallas kernels  32.3 us (80%)
  local copies, waits for them, and re-layouts  5.84 us (14%)
  between operations  1.95 us (5%)
    pallas_call x1, Pallas kernels, on_device(): pl.pallas_call(kernel, out_shape=(like(pre_q), like(roll_q), like(pre_q),...  32.3 us
    unnamed x16, local copies, waits for them, and re-layouts  5.84 us

profile of v1, /device:TPU:1, one launch (start us, length us, event | category | flops | bytes accessed | tf_op | source)
XLA Modules:
  0.0 40.1 jit_solution(524188531344927011)
XLA Ops:
  1.9 32.3 %shard_map.127 = (bf16[64,1024]{1,0:T(8,128)(2,1)}, bf16[1,128,1024]{2,1,0:T(8,128)(2,1)}, bf16[64,1024]{1,0:T(8,128)(2,1)}, bf16[1,128,1024]{2,1,0:T(8,128)(2,1...) custom-call(s32[1]{0:T(128)S(6)} %copy.20.pre_len_ref, s32[1]{0:T(128)S(6)} %copy.21.roll_len_ref, ...), custom_call_target="tpu_custom_call" | custom-call | tf_op jit(solution)/shard_map/pallas_call | solution.py:366
  34.2 0.0 copy-start.1
  34.2 1.6 %copy.22 = bf16[64,1024]{1,0:T(8,128)(2,1)} copy(bf16[64,1024]{1,0:T(8,128)(2,1)} %get-tuple-element.12) | data formatting | bytes 262144
  35.8 0.0 copy-done.1
  35.8 0.0 copy-start.2
  35.8 0.7 %copy.23 = bf16[1,128,1024]{2,1,0:T(8,128)(2,1)} copy(bf16[1,128,1024]{2,1,0:T(8,128)(2,1)S(1)} %copy-done.1) | data formatting | bytes 524288
  36.5 0.3 copy-done.2
  36.8 0.0 copy-start
  36.8 0.7 %copy.24 = bf16[64,1024]{1,0:T(8,128)(2,1)} copy(bf16[64,1024]{1,0:T(8,128)(2,1)S(1)} %copy-done.2) | data formatting | bytes 262144
  37.5 0.3 copy-done
  37.8 0.0 copy-start.4
  37.8 0.7 %copy.25 = bf16[1,128,1024]{2,1,0:T(8,128)(2,1)} copy(bf16[1,128,1024]{2,1,0:T(8,128)(2,1)S(1)} %copy-done) | data formatting | bytes 524288
  38.5 0.1 copy-done.4
  38.6 0.0 copy-start.3
  38.6 0.6 %copy.26 = bf16[64,256]{1,0:T(8,128)(2,1)} copy(bf16[64,256]{1,0:T(8,128)(2,1)S(1)} %copy-done.4) | data formatting | bytes 65536
  39.2 0.2 copy-done.3
  39.4 0.6 %copy.27 = bf16[1,128,256]{2,1,0:T(8,128)(2,1)} copy(bf16[1,128,256]{2,1,0:T(8,128)(2,1)S(1)} %copy-done.3) | data formatting | bytes 131072
Async XLA Ops:
  34.2 1.6 %copy-start.1 = (bf16[1,128,1024]{2,1,0:T(8,128)(2,1)S(1)}, bf16[1,128,1024]{2,1,0:T(8,128)(2,1)}, u32[]{:S(2)}) copy-start(bf16[1,128,1024]{2,1,0:T(8,128)(2,1)} %get-tuple-element.13) | copy-start | bytes 786436
  35.8 1.0 %copy-start.2 = (bf16[64,1024]{1,0:T(8,128)(2,1)S(1)}, bf16[64,1024]{1,0:T(8,128)(2,1)}, u32[]{:S(2)}) copy-start(bf16[64,1024]{1,0:T(8,128)(2,1)} %get-tuple-element.14) | copy-start | bytes 393220
  36.8 1.0 %copy-start = (bf16[1,128,1024]{2,1,0:T(8,128)(2,1)S(1)}, bf16[1,128,1024]{2,1,0:T(8,128)(2,1)}, u32[]{:S(2)}) copy-start(bf16[1,128,1024]{2,1,0:T(8,128)(2,1)} %get-tuple-element.15) | copy-start | bytes 786436
  37.8 0.8 %copy-start.4 = (bf16[64,256]{1,0:T(8,128)(2,1)S(1)}, bf16[64,256]{1,0:T(8,128)(2,1)}, u32[]{:S(2)}) copy-start(bf16[64,256]{1,0:T(8,128)(2,1)} %get-tuple-element.16) | copy-start | bytes 98308
  38.6 0.9 %copy-start.3 = (bf16[1,128,256]{2,1,0:T(8,128)(2,1)S(1)}, bf16[1,128,256]{2,1,0:T(8,128)(2,1)}, u32[]{:S(2)}) copy-start(bf16[1,128,256]{2,1,0:T(8,128)(2,1)} %get-tuple-element.17) | copy-start | bytes 196612

commit v2 on v1

--- a/solution.py
+++ b/solution.py
@@ -356,14 +356,28 @@
         copy.wait_send()
 
 
+def drain(*refs):
+    count = (len(refs) - 1) // 2
+    sem = refs[-1]
+    copies = [
+        pltpu.make_async_copy(refs[index], refs[count + index], sem.at[index])
+        for index in range(count)
+    ]
+    for copy in copies:
+        copy.start()
+    for copy in copies:
+        copy.wait()
+
+
 def on_device(pre_q, pre_kv, roll_q, roll_kv, pre_grad, roll_grad, pre_len, roll_len):
     smem = pl.BlockSpec(memory_space=pltpu.SMEM)
     vmem = pl.BlockSpec(memory_space=pltpu.VMEM)
     anywhere = pl.BlockSpec(memory_space=pl.ANY)
-    like = lambda array: jax.ShapeDtypeStruct(array.shape, BF16)
+    like = lambda array: pltpu.VMEM(array.shape, BF16)
+    final = lambda array: jax.ShapeDtypeStruct(array.shape, BF16)
     copies = GROUP
     sums = CORES + HALVES * ROW + 1
-    return pl.pallas_call(
+    results = pl.pallas_call(
         kernel,
         out_shape=(
             like(pre_q),
@@ -406,6 +420,13 @@
             collective_id=0, has_side_effects=True, vmem_limit_bytes=56 << 20
         ),
     )(pre_len, roll_len, pre_q, pre_kv, roll_q, roll_kv, pre_grad, roll_grad)
+    return pl.pallas_call(
+        drain,
+        out_shape=tuple(final(array) for array in (pre_q, roll_q, pre_q, roll_q, pre_kv, roll_kv)),
+        in_specs=[vmem] * 6,
+        out_specs=[anywhere] * 6,
+        scratch_shapes=[pltpu.SemaphoreType.DMA((6,))],
+    )(*(pltpu.with_memory_space_constraint(result, pltpu.VMEM) for result in results))
 
 
 def solution(mesh):

time: 40.4 us -> 34.4 us (0.85)
  local copies, waits for them, and re-layouts: 5.84 us -> 0 us
    unnamed x16 -> x0, local copies, waits for them, and re-layouts: 5.84 us -> none
    pallas_call x0 -> x1, Pallas kernels: none -> 0.95 us  [on_device(): pl.pallas_call(drain, out_shape=tuple((final(array) for array in (pre_q,...]
    pallas_call x1, Pallas kernels: 32.3 us -> 31.4 us  [on_device(): pl.pallas_call(kernel, out_shape=(like(pre_q), like(roll_q), like(pre_q),...]
where the time goes in v2:
time: 34.4 us; the launch traced here: 34.2 us
  Pallas kernels  32.3 us (94%)
  between operations  1.93 us (6%)
    pallas_call x1, Pallas kernels, on_device(): pl.pallas_call(kernel, out_shape=(like(pre_q), like(roll_q), like(pre_q),...  31.4 us
    pallas_call x1, Pallas kernels, on_device(): pl.pallas_call(drain, out_shape=tuple((final(array) for array in (pre_q,...  0.95 us

profile of v2, /device:TPU:1, one launch (start us, length us, event | category | flops | bytes accessed | tf_op | source)
XLA Modules:
  0.0 34.2 jit_solution(16511888294339287529)
XLA Ops:
  1.9 31.4 %shard_map.127 = (bf16[64,1024]{1,0:T(8,128)(2,1)S(1)}, bf16[1,128,1024]{2,1,0:T(8,128)(2,1)S(1)}, bf16[64,1024]{1,0:T(8,128)(2,1)S(1)}, bf16[1,128,1024]{2,1,0:...) custom-call(s32[1]{0:T(128)S(6)} %copy.14.pre_len_ref, s32[1]{0:T(128)S(6)} %copy.15.roll_len_ref, ...), custom_call_target="tpu_custom_call" | custom-call | tf_op jit(solution)/shard_map/pallas_call | solution.py:380
  33.3 1.0 %shard_map.128 = (bf16[64,1024]{1,0:T(8,128)(2,1)}, bf16[1,128,1024]{2,1,0:T(8,128)(2,1)}, bf16[64,1024]{1,0:T(8,128)(2,1)}, bf16[1,128,1024]{2,1,0:T(8,128)(2,1...) custom-call(bf16[64,1024]{1,0:T(8,128)(2,1)S(1)} %get-tuple-element.12.refs_0_, ...), custom_call_target="tpu_custom_call" | custom-call | tf_op jit(solution)/shard_map/pallas_call | solution.py:423

commit v3 on v2

v3 whole, which is shorter than its diff:
```python
import functools

import jax
import jax.numpy as jnp
from jax import lax
from jax.experimental import pallas as pl
from jax.experimental.pallas import tpu as pltpu
from jax.sharding import PartitionSpec as P

F32 = jnp.float32
BF16 = jnp.bfloat16
MESH = pl.DeviceIdType.MESH
masked_score = -1e30
HALVES, ROW, CORES = 2, 4, 2
BLOCK = 64
RESP = 128
HEADS = 8
HD = 128
GROUP = HALVES * ROW * CORES
PREFIX = GROUP * BLOCK
ROLL_ROWS = HEADS * RESP
ROWS = HEADS * (RESP + BLOCK)
SCALE = HD**-0.5
LOG2E = 1.4426950408889634


def dot(left, right, left_dim, right_dim):
    return lax.dot_general(
        left, right, (((left_dim,), (right_dim,)), ((), ())), preferred_element_type=F32
    )


POS = (0, 1, 3, 2)


def slot(half, place, core):
    return (half * ROW + POS[place]) * CORES + core


def rows_of(half, place, core):
    return pl.ds(slot(half, place, core) * BLOCK, BLOCK)


def fold8(values, combine):
    return combine(values.reshape(values.shape[0] // 8, 8, values.shape[1]), axis=0)


def kernel(
    pre_len_ref,
    roll_len_ref,
    pre_q,
    pre_kv,
    roll_q,
    roll_kv,
    pre_grad,
    roll_grad,
    pre_out,
    roll_out,
    pre_dq,
    roll_dq,
    pre_dkv,
    roll_dkv,
    rq,
    rg,
    pq,
    pg,
    rkv,
    kvs,
    queries,
    grads,
    score,
    weight,
    gradp,
    keys_t,
    vals_t,
    to_core,
    from_core,
    own_sum,
    to_owner,
    from_owner,
    load_sem,
    send_sem,
    recv_sem,
    sum_send_sem,
    sum_recv_sem,
):
    me = lax.axis_index("roll")
    my_half, my_place, my_core = me // (ROW * CORES), (me // CORES) % ROW, me % CORES

    def device(half, place, core):
        return (
            ((my_half + half) % HALVES) * (ROW * CORES)
            + ((my_place + place) % ROW) * CORES
            + (my_core + core) % CORES
        )

    partners = [(1, 0, 0), (0, 0, 1), (0, 1, 0), (0, 3, 0), (0, 2, 0)]
    barrier = pltpu.get_barrier_semaphore()
    for partner in partners:
        pl.semaphore_signal(
            barrier, inc=1, device_id={"roll": device(*partner)}, device_id_type=MESH
        )

    loads = []
    for index, (source, target) in enumerate(
        (
            (pre_kv, kvs.at[rows_of(0, 0, 0)]),
            (roll_kv.at[0], rkv),
            (roll_q.at[0], rq),
            (pre_q, pq),
            (roll_grad.at[0], rg),
            (pre_grad, pg),
        )
    ):
        loads.append(pltpu.make_async_copy(source, target, load_sem.at[index]))
        loads[-1].start()

    copies = {}

    def push(source, block, to):
        at = slot(*block)
        copies[block] = pltpu.make_async_remote_copy(
            src_ref=source,
            dst_ref=kvs.at[rows_of(*block)],
            send_sem=send_sem.at[at],
            recv_sem=recv_sem.at[at],
            device_id={"roll": device(*to)},
            device_id_type=MESH,
        )
        copies[block].start()

    def relay(half, place):
        push(kvs.at[rows_of(half, place, 0)], (half, place, 1), (0, 0, 1))

    loads[0].wait()
    pl.semaphore_wait(barrier, len(partners))
    held = kvs.at[rows_of(0, 0, 0)]
    push(held, (1, 0, 0), (1, 0, 0))
    for place in (2, 1, 3):
        push(held, (0, ROW - place, 0), (0, place, 0))
    push(held, (0, 0, 1), (0, 0, 1))

    pre_len = pre_len_ref[0]
    roll_len = roll_len_ref[0]
    lane = lax.broadcasted_iota(jnp.int32, (1, ROWS), 1)
    is_roll = lane < ROLL_ROWS
    query_pos = me * BLOCK + lane % BLOCK
    limit = jnp.where(is_roll, pre_len - 1, jnp.minimum(query_pos, pre_len - 1))
    own_limit = jnp.minimum(lane[:, :ROLL_ROWS] % RESP, roll_len - 1)
    rows_left = jnp.where(is_roll, roll_len - lane % RESP, pre_len - query_pos)

    for load in loads[1:]:
        load.wait()
    for head in range(HEADS):
        columns = slice(head * HD, (head + 1) * HD)
        at = pl.ds(head * RESP, RESP)
        queries[at, :] = rq[:, columns]
        grads[at, :] = rg[:, columns]
        at = pl.ds(ROLL_ROWS + head * BLOCK, BLOCK)
        queries[at, :] = pq[:, columns]
        grads[at, :] = pg[:, columns]

    own_rows = pl.ds(PREFIX, RESP)
    all_cols = slice(0, ROWS)
    own_cols = slice(0, ROLL_ROWS)

    def take(first, count):
        at = pl.ds(first, count)
        keys_t[:, at] = kvs[at, 0:HD].T
        vals_t[:, at] = kvs[at, HD : 2 * HD].T
        row = lax.broadcasted_iota(jnp.int32, (count, 1), 0) + first
        half = row // (PREFIX // HALVES)
        order = row // (CORES * BLOCK) % ROW
        place = order ^ (order >> 1)
        core = row // BLOCK % CORES
        owner = (
            ((my_half + half) % HALVES) * (ROW * CORES)
            + ((my_place + place) % ROW) * CORES
            + (my_core + core) % CORES
        )
        key_pos = owner * BLOCK + row % BLOCK
        logits = dot(kvs[at, 0:HD], queries[...], 1, 1) * (SCALE * LOG2E)
        logits = jnp.where(key_pos <= limit, logits, masked_score)
        score[at, :] = logits
        return fold8(logits, jnp.max)

    def widen(total, own, combine):
        return jnp.concatenate([combine(total[:, own_cols], own), total[:, ROLL_ROWS:]], axis=1)

    def weigh(at, cols, row_max):
        expo = jnp.exp2(score[at, cols] - row_max)
        rounded = expo.astype(BF16)
        weight[at, cols] = rounded
        return fold8(expo, jnp.sum), dot(vals_t[:, at], rounded, 1, 0)

    def grad_probs_of(at):
        return dot(kvs[at, HD : 2 * HD], grads[...], 1, 1)

    own_key = lax.broadcasted_iota(jnp.int32, (RESP, 1), 0)
    own_logits = dot(rkv[:, 0:HD], queries[own_cols, :], 1, 1) * (SCALE * LOG2E)
    own_logits = jnp.where(own_key <= own_limit, own_logits, masked_score)
    score[own_rows, own_cols] = own_logits
    own_max = fold8(own_logits, jnp.max)
    keys_t[:, own_rows] = rkv[:, 0:HD].T
    vals_t[:, own_rows] = rkv[:, HD : 2 * HD].T
    gradp[own_rows, own_cols] = dot(rkv[:, HD : 2 * HD], grads[own_cols, :], 1, 1)
    grad_t = grads[...].T.astype(F32)

    pair = CORES * BLOCK
    for place in (1, 3, 2):
        copies[0, place, 0].wait_recv()
        relay(0, place)
    copies[0, 0, 1].wait_recv()
    copies[0, 1, 1].wait_recv()
    near_max = take(0, 2 * pair)
    copies[1, 0, 0].wait_recv()
    for place in (2, 1, 3):
        push(kvs.at[rows_of(1, 0, 0)], (1, ROW - place, 0), (0, place, 0))
    relay(1, 0)
    copies[0, 3, 1].wait_recv()
    copies[0, 2, 1].wait_recv()
    near_max = jnp.maximum(near_max, take(2 * pair, 2 * pair))
    near_max = widen(near_max, own_max, jnp.maximum)
    row_max = jnp.max(near_max, axis=0, keepdims=True)
    near = pl.ds(0, ROW * pair)
    row_sum, out_t = weigh(near, all_cols, row_max)
    own_sum_8, own_out = weigh(own_rows, own_cols, row_max[:, own_cols])
    row_sum = jnp.sum(widen(row_sum, own_sum_8, jnp.add), axis=0, keepdims=True)
    out_t = widen(out_t, own_out, jnp.add)
    phase_max = [row_max]
    gradp[near, :] = grad_probs_of(near)

    def fold_in(first, count, state):
        row_max, row_sum, out_t = state
        new_max = jnp.max(take(first, count), axis=0, keepdims=True)
        new_max = jnp.maximum(row_max, new_max)
        shrink = jnp.exp2(row_max - new_max)
        more_sum, more_out = weigh(pl.ds(first, count), all_cols, new_max)
        phase_max.append(new_max)
        row_sum = row_sum * shrink + jnp.sum(more_sum, axis=0, keepdims=True)
        return new_max, row_sum, out_t * shrink + more_out

    far = ROW * pair
    copies[1, 0, 1].wait_recv()
    state = fold_in(far, pair, (row_max, row_sum, out_t))
    gradp[pl.ds(far, pair), :] = grad_probs_of(pl.ds(far, pair))
    for place in (1, 3, 2):
        copies[1, place, 0].wait_recv()
        relay(1, place)
    copies[1, 1, 1].wait_recv()
    copies[1, 3, 1].wait_recv()
    state = fold_in(far + pair, 2 * pair, state)
    copies[1, 2, 1].wait_recv()
    row_max, row_sum, out_t = fold_in(far + 3 * pair, pair, state)

    inverse = jnp.where(rows_left > 0, 1.0 / row_sum, 0.0)
    out_t = (out_t * inverse).astype(BF16)
    row_dot = jnp.sum(grad_t * out_t.astype(F32), axis=0, keepdims=True)
    factors = [jnp.exp2(past - row_max) * inverse for past in phase_max]

    def back(at, cols, grad_probs, factor):
        probs = weight[at, cols].astype(F32) * factor[:, cols]
        grad_logits = (probs * (grad_probs - row_dot[:, cols])).astype(BF16)
        weight[at, cols] = grad_logits
        grad_vals = dot(probs.astype(BF16), grads[cols, :], 1, 0)
        grad_keys = dot(grad_logits, queries[cols, :], 1, 0) * SCALE
        return grad_keys, grad_vals

    def ship(source, target, index, to):
        copy = pltpu.make_async_remote_copy(
            src_ref=source,
            dst_ref=target,
            send_sem=sum_send_sem.at[index],
            recv_sem=sum_recv_sem.at[index],
            device_id={"roll": device(*to)},
            device_id_type=MESH,
        )
        copy.start()
        return copy

    sums = {}

    def prefix_back(first, count, grad_probs, factor):
        grad_keys, grad_vals = back(pl.ds(first, count), all_cols, grad_probs, factor)
        for pairs in range(count // pair):
            at = first // pair + pairs
            rows = slice(pairs * pair, pairs * pair + BLOCK)
            own_sum[at, :, 0:HD] = grad_keys[rows]
            own_sum[at, :, HD : 2 * HD] = grad_vals[rows]
            rows = slice(pairs * pair + BLOCK, (pairs + 1) * pair)
            to_core[at, :, 0:HD] = grad_keys[rows].astype(BF16)
            to_core[at, :, HD : 2 * HD] = grad_vals[rows].astype(BF16)
            sums["core", at] = ship(to_core.at[at], from_core.at[at], at, (0, 0, 1))

    def chip_total(at):
        sums["core", at].wait_recv()
        return own_sum[at] + from_core[at].astype(F32)

    def send_on(half, place, to):
        at = half * ROW + POS[place]
        to_owner[at] = chip_total(at).astype(BF16)
        lands = half * ROW + POS[(ROW - place) % ROW]
        sums["owner", lands] = ship(
            to_owner.at[at], from_owner.at[lands], HALVES * ROW + lands, to
        )

    last = pl.ds(far + 3 * pair, pair)
    middle = pl.ds(far + pair, 2 * pair)
    prefix_back(far + pair, 2 * pair, grad_probs_of(middle), factors[2])
    prefix_back(far + 3 * pair, pair, grad_probs_of(last), factors[3])
    send_on(1, 1, (0, 1, 0))
    send_on(1, 3, (0, 3, 0))
    prefix_back(far, pair, gradp[pl.ds(far, pair), :], factors[1])
    send_on(1, 2, (1, 2, 0))
    prefix_back(2 * pair, 2 * pair, gradp[pl.ds(2 * pair, 2 * pair), :], factors[0])
    prefix_back(0, 2 * pair, gradp[pl.ds(0, 2 * pair), :], factors[0])
    send_on(0, 2, (0, 2, 0))
    send_on(0, 3, (0, 3, 0))
    send_on(0, 1, (0, 1, 0))

    total = chip_total(ROW)
    for place in (1, 3):
        at = ROW + POS[place]
        sums["owner", at].wait_recv()
        total = total + from_owner[at].astype(F32)
    to_owner[ROW] = total.astype(BF16)
    sums["owner", ROW] = ship(
        to_owner.at[ROW], from_owner.at[ROW], HALVES * ROW + ROW, (1, 0, 0)
    )

    grad_keys, grad_vals = back(
        own_rows, own_cols, gradp[own_rows, own_cols], factors[0]
    )
    roll_dkv[0, :, 0:HD] = grad_keys.astype(BF16)
    roll_dkv[0, :, HD : 2 * HD] = grad_vals.astype(BF16)
    out = out_t.T
    for head in range(HEADS):
        columns = slice(head * HD, (head + 1) * HD)
        roll_out[0, :, columns] = out[head * RESP : (head + 1) * RESP]
        at = ROLL_ROWS + head * BLOCK
        pre_out[:, columns] = out[at : at + BLOCK]
    grad_query = dot(keys_t[:, 0:PREFIX], weight[0:PREFIX, :], 1, 0)
    grad_query = widen(
        grad_query, dot(keys_t[:, own_rows], weight[own_rows, own_cols], 1, 0), jnp.add
    )
    grad_query = (grad_query * SCALE).astype(BF16).T
    for head in range(HEADS):
        columns = slice(head * HD, (head + 1) * HD)
        roll_dq[0, :, columns] = grad_query[head * RESP : (head + 1) * RESP]
        at = ROLL_ROWS + head * BLOCK
        pre_dq[:, columns] = grad_query[at : at + BLOCK]

    total = chip_total(0)
    for at in (1, 2, 3, ROW + POS[2], ROW):
        sums["owner", at].wait_recv()
        total = total + from_owner[at].astype(F32)
    pre_dkv[...] = total.astype(BF16)
    for copy in (*copies.values(), *sums.values()):
        copy.wait_send()


def drain(*refs):
    count = (len(refs) - 1) // 2
    sem = refs[-1]
    copies = [
        pltpu.make_async_copy(refs[index], refs[count + index], sem.at[index])
        for index in range(count)
    ]
    for copy in copies:
        copy.start()
    for copy in copies:
        copy.wait()


def on_device(pre_q, pre_kv, roll_q, roll_kv, pre_grad, roll_grad, pre_len, roll_len):
    smem = pl.BlockSpec(memory_space=pltpu.SMEM)
    vmem = pl.BlockSpec(memory_space=pltpu.VMEM)
    anywhere = pl.BlockSpec(memory_space=pl.ANY)
    like = lambda array: pltpu.VMEM(array.shape, BF16)
    final = lambda array: jax.ShapeDtypeStruct(array.shape, BF16)
    copies = GROUP
    sums = 2 * HALVES * ROW
    results = pl.pallas_call(
        kernel,
        out_shape=(
            like(pre_q),
            like(roll_q),
            like(pre_q),
            like(roll_q),
            like(pre_kv),
            like(roll_kv),
        ),
        in_specs=[smem] * 2 + [anywhere] * 6,
        out_specs=[vmem] * 6,
        scratch_shapes=[
            pltpu.VMEM((RESP, HEADS * HD), BF16),
            pltpu.VMEM((RESP, HEADS * HD), BF16),
            pltpu.VMEM((BLOCK, HEADS * HD), BF16),
            pltpu.VMEM((BLOCK, HEADS * HD), BF16),
            pltpu.VMEM((RESP, 2 * HD), BF16),
            pltpu.VMEM((PREFIX, 2 * HD), BF16),
            pltpu.VMEM((ROWS, HD), BF16),
            pltpu.VMEM((ROWS, HD), BF16),
            pltpu.VMEM((PREFIX + RESP, ROWS), F32),
            pltpu.VMEM((PREFIX + RESP, ROWS), BF16),
            pltpu.VMEM((PREFIX + RESP, ROWS), F32),
            pltpu.VMEM((HD, PREFIX + RESP), BF16),
            pltpu.VMEM((HD, PREFIX + RESP), BF16),
            pltpu.VMEM((HALVES * ROW, BLOCK, 2 * HD), BF16),
            pltpu.VMEM((HALVES * ROW, BLOCK, 2 * HD), BF16),
            pltpu.VMEM((HALVES * ROW, BLOCK, 2 * HD), F32),
            pltpu.VMEM((HALVES * ROW, BLOCK, 2 * HD), BF16),
            pltpu.VMEM((HALVES * ROW, BLOCK, 2 * HD), BF16),
            pltpu.SemaphoreType.DMA((6,)),
            pltpu.SemaphoreType.DMA((copies,)),
            pltpu.SemaphoreType.DMA((copies,)),
            pltpu.SemaphoreType.DMA((sums,)),
            pltpu.SemaphoreType.DMA((sums,)),
        ],
        compiler_params=pltpu.CompilerParams(
            collective_id=0, has_side_effects=True, vmem_limit_bytes=56 << 20
        ),
    )(pre_len, roll_len, pre_q, pre_kv, roll_q, roll_kv, pre_grad, roll_grad)
    return pl.pallas_call(
        drain,
        out_shape=tuple(final(array) for array in (pre_q, roll_q, pre_q, roll_q, pre_kv, roll_kv)),
        in_specs=[vmem] * 6,
        out_specs=[anywhere] * 6,
        scratch_shapes=[pltpu.SemaphoreType.DMA((6,))],
    )(*(pltpu.with_memory_space_constraint(result, pltpu.VMEM) for result in results))


def solution(mesh):
    in_specs = (
        P(("prompt", "roll"), None),
        P(("prompt", "roll"), None),
        P(("prompt", "roll"), None, None),
        P(("prompt", "roll"), None, None),
        P(("prompt", "roll"), None),
        P(("prompt", "roll"), None, None),
        P("prompt"),
        P(("prompt", "roll")),
    )
    out_specs = (
        P(("prompt", "roll"), None),
        P(("prompt", "roll"), None, None),
        P(("prompt", "roll"), None),
        P(("prompt", "roll"), None, None),
        P(("prompt", "roll"), None),
        P(("prompt", "roll"), None, None),
    )
    return jax.shard_map(
        on_device, mesh=mesh, in_specs=in_specs, out_specs=out_specs, check_vma=False
    )
```

time: 34.4 us -> 33.7 us (0.980)
  Pallas kernels: 32.3 us -> 31.7 us
    pallas_call x1, Pallas kernels: 31.4 us -> 30.7 us  [on_device(): pl.pallas_call(kernel, out_shape=(like(pre_q), like(roll_q), like(pre_q),...]
where the time goes in v3:
time: 33.7 us; the launch traced here: 33.6 us
  Pallas kernels  31.7 us (94%)
  between operations  1.93 us (6%)
    pallas_call x1, Pallas kernels, on_device(): pl.pallas_call(kernel, out_shape=(like(pre_q), like(roll_q), like(pre_q),...  30.7 us
    pallas_call x1, Pallas kernels, on_device(): pl.pallas_call(drain, out_shape=tuple((final(array) for array in (pre_q,...  0.95 us

profile of v3, /device:TPU:1, one launch (start us, length us, event | category | flops | bytes accessed | tf_op | source)
XLA Modules:
  0.0 33.6 jit_solution(13918684642885601389)
XLA Ops:
  1.9 30.7 %shard_map.127 = (bf16[64,1024]{1,0:T(8,128)(2,1)S(1)}, bf16[1,128,1024]{2,1,0:T(8,128)(2,1)S(1)}, bf16[64,1024]{1,0:T(8,128)(2,1)S(1)}, bf16[1,128,1024]{2,1,0:...) custom-call(s32[1]{0:T(128)S(6)} %copy.14.pre_len_ref, s32[1]{0:T(128)S(6)} %copy.15.roll_len_ref, ...), custom_call_target="tpu_custom_call" | custom-call | tf_op jit(solution)/shard_map/pallas_call | solution.py:383
  32.6 1.0 %shard_map.128 = (bf16[64,1024]{1,0:T(8,128)(2,1)}, bf16[1,128,1024]{2,1,0:T(8,128)(2,1)}, bf16[64,1024]{1,0:T(8,128)(2,1)}, bf16[1,128,1024]{2,1,0:T(8,128)(2,1...) custom-call(bf16[64,1024]{1,0:T(8,128)(2,1)S(1)} %get-tuple-element.12.refs_0_, ...), custom_call_target="tpu_custom_call" | custom-call | tf_op jit(solution)/shard_map/pallas_call | solution.py:424

commit v4 on v3

--- a/solution.py
+++ b/solution.py
@@ -31,10 +31,16 @@
 
 
 POS = (0, 1, 3, 2)
+LAYOUT = ((0, 0), (0, 1), (1, 0), (3, 0), (1, 1), (3, 1), (2, 0), (2, 1))
 
 
 def slot(half, place, core):
-    return (half * ROW + POS[place]) * CORES + core
+    return half * len(LAYOUT) + LAYOUT.index((place, core))
+
+
+def blocks_in(first, count):
+    slots = range(first // BLOCK, (first + count) // BLOCK)
+    return [(at // len(LAYOUT), *LAYOUT[at % len(LAYOUT)]) for at in slots]
 
 
 def rows_of(half, place, core):
@@ -78,6 +84,8 @@
     own_sum,
     to_owner,
     from_owner,
+    from_row,
+    to_opposite,
     load_sem,
     send_sem,
     recv_sem,
@@ -94,12 +102,21 @@
             + (my_core + core) % CORES
         )
 
-    partners = [(1, 0, 0), (0, 0, 1), (0, 1, 0), (0, 3, 0), (0, 2, 0)]
+    speaker = 1 - my_core
+    partners = [(1, 0, speaker), (0, 0, 1), (0, 1, 0), (0, 3, 0), (0, 2, 0)]
     barrier = pltpu.get_barrier_semaphore()
-    for partner in partners:
+
+    def announce(partner):
         pl.semaphore_signal(
             barrier, inc=1, device_id={"roll": device(*partner)}, device_id_type=MESH
         )
+
+    for partner in partners:
+        announce(partner)
+
+    @pl.when(my_core == 1)
+    def _():
+        announce((1, 0, 1))
 
     loads = []
     for index, (source, target) in enumerate(
@@ -115,30 +132,49 @@
         loads.append(pltpu.make_async_copy(source, target, load_sem.at[index]))
         loads[-1].start()
 
-    copies = {}
-
-    def push(source, block, to):
-        at = slot(*block)
-        copies[block] = pltpu.make_async_remote_copy(
+    def block_copy(source, at, index, to):
+        return pltpu.make_async_remote_copy(
             src_ref=source,
-            dst_ref=kvs.at[rows_of(*block)],
-            send_sem=send_sem.at[at],
+            dst_ref=kvs.at[pl.ds(at * BLOCK, BLOCK)],
+            send_sem=send_sem.at[index],
             recv_sem=recv_sem.at[at],
             device_id={"roll": device(*to)},
             device_id_type=MESH,
         )
-        copies[block].start()
-
-    def relay(half, place):
-        push(kvs.at[rows_of(half, place, 0)], (half, place, 1), (0, 0, 1))
-
+
+    def push(source, at, index, to):
+        copy = block_copy(source, at, index, to)
+        copy.start()
+        return copy
+
+    def arrived(*block):
+        at = slot(*block)
+        block_copy(kvs.at[rows_of(*block)], at, 0, (0, 0, 1)).wait_recv()
+
+    def relay_near(place):
+        at = slot(0, place, 1)
+        copies.append(push(kvs.at[rows_of(0, place, 0)], at, at, (0, 0, 1)))
+
+    def to_sibling(place, core, start=True):
+        at = slot(1, place, 1 - core)
+        copy = block_copy(kvs.at[rows_of(1, place, core)], at, GROUP + at, (0, 0, 1))
+        copy.start() if start else copy.wait_send()
+
+    def along_row(place, core, start=True):
+        at = slot(1, ROW - place, core)
+        copy = block_copy(kvs.at[rows_of(1, 0, core)], at, GROUP + place * CORES + core, (0, place, 0))
+        copy.start() if start else copy.wait_send()
+
+    copies = []
     loads[0].wait()
-    pl.semaphore_wait(barrier, len(partners))
+    pl.semaphore_wait(barrier, len(partners) + my_core)
     held = kvs.at[rows_of(0, 0, 0)]
-    push(held, (1, 0, 0), (1, 0, 0))
+    copies.append(push(held, slot(1, 0, 0) + speaker, 0, (1, 0, speaker)))
     for place in (2, 1, 3):
-        push(held, (0, ROW - place, 0), (0, place, 0))
-    push(held, (0, 0, 1), (0, 0, 1))
+        at = slot(0, ROW - place, 0)
+        copies.append(push(held, at, at, (0, place, 0)))
+    at = slot(0, 0, 1)
+    copies.append(push(held, at, at, (0, 0, 1)))
 
     pre_len = pre_len_ref[0]
     roll_len = roll_len_ref[0]
@@ -168,17 +204,11 @@
         at = pl.ds(first, count)
         keys_t[:, at] = kvs[at, 0:HD].T
         vals_t[:, at] = kvs[at, HD : 2 * HD].T
-        row = lax.broadcasted_iota(jnp.int32, (count, 1), 0) + first
-        half = row // (PREFIX // HALVES)
-        order = row // (CORES * BLOCK) % ROW
-        place = order ^ (order >> 1)
-        core = row // BLOCK % CORES
-        owner = (
-            ((my_half + half) % HALVES) * (ROW * CORES)
-            + ((my_place + place) % ROW) * CORES
-            + (my_core + core) % CORES
-        )
-        key_pos = owner * BLOCK + row % BLOCK
+        row = lax.broadcasted_iota(jnp.int32, (count, 1), 0)
+        base = 0
+        for index, block in enumerate(blocks_in(first, count)):
+            base = jnp.where(row // BLOCK == index, device(*block) * BLOCK, base)
+        key_pos = base + row % BLOCK
         logits = dot(kvs[at, 0:HD], queries[...], 1, 1) * (SCALE * LOG2E)
         logits = jnp.where(key_pos <= limit, logits, masked_score)
         score[at, :] = logits
@@ -208,17 +238,23 @@
 
     pair = CORES * BLOCK
     for place in (1, 3, 2):
-        copies[0, place, 0].wait_recv()
-        relay(0, place)
-    copies[0, 0, 1].wait_recv()
-    copies[0, 1, 1].wait_recv()
+        arrived(0, place, 0)
+        relay_near(place)
+    arrived(0, 0, 1)
     near_max = take(0, 2 * pair)
-    copies[1, 0, 0].wait_recv()
-    for place in (2, 1, 3):
-        push(kvs.at[rows_of(1, 0, 0)], (1, ROW - place, 0), (0, place, 0))
-    relay(1, 0)
-    copies[0, 3, 1].wait_recv()
-    copies[0, 2, 1].wait_recv()
+
+    @pl.when(my_core == 1)
+    def _():
+        for core in range(CORES):
+            arrived(1, 0, core)
+        for place in (2, 1, 3):
+            for core in range(CORES):
+                along_row(place, core)
+        for core in range(CORES):
+            to_sibling(0, core)
+
+    for place in (1, 3, 2):
+        arrived(0, place, 1)
     near_max = jnp.maximum(near_max, take(2 * pair, 2 * pair))
     near_max = widen(near_max, own_max, jnp.maximum)
     row_max = jnp.max(near_max, axis=0, keepdims=True)
@@ -241,16 +277,28 @@
         return new_max, row_sum, out_t * shrink + more_out
 
     far = ROW * pair
-    copies[1, 0, 1].wait_recv()
+
+    @pl.when(my_core == 0)
+    def _():
+        for core in range(CORES):
+            arrived(1, 0, core)
+
     state = fold_in(far, pair, (row_max, row_sum, out_t))
     gradp[pl.ds(far, pair), :] = grad_probs_of(pl.ds(far, pair))
-    for place in (1, 3, 2):
-        copies[1, place, 0].wait_recv()
-        relay(1, place)
-    copies[1, 1, 1].wait_recv()
-    copies[1, 3, 1].wait_recv()
+    def hear(*places):
+        for place in places:
+            for core in range(CORES):
+                arrived(1, place, core)
+
+        @pl.when(my_core == 1)
+        def _():
+            for place in places:
+                for core in range(CORES):
+                    to_sibling(place, core)
+
+    hear(1, 3)
     state = fold_in(far + pair, 2 * pair, state)
-    copies[1, 2, 1].wait_recv()
+    hear(2)
     row_max, row_sum, out_t = fold_in(far + 3 * pair, pair, state)
 
     inverse = jnp.where(rows_left > 0, 1.0 / row_sum, 0.0)
@@ -266,15 +314,18 @@
         grad_keys = dot(grad_logits, queries[cols, :], 1, 0) * SCALE
         return grad_keys, grad_vals
 
-    def ship(source, target, index, to):
-        copy = pltpu.make_async_remote_copy(
+    def term_copy(source, target, sent, landed, to):
+        return pltpu.make_async_remote_copy(
             src_ref=source,
             dst_ref=target,
-            send_sem=sum_send_sem.at[index],
-            recv_sem=sum_recv_sem.at[index],
+            send_sem=sum_send_sem.at[sent],
+            recv_sem=sum_recv_sem.at[landed],
             device_id={"roll": device(*to)},
             device_id_type=MESH,
         )
+
+    def ship(source, target, index, to):
+        copy = term_copy(source, target, index, index, to)
         copy.start()
         return copy
 
@@ -282,15 +333,16 @@
 
     def prefix_back(first, count, grad_probs, factor):
         grad_keys, grad_vals = back(pl.ds(first, count), all_cols, grad_probs, factor)
-        for pairs in range(count // pair):
-            at = first // pair + pairs
-            rows = slice(pairs * pair, pairs * pair + BLOCK)
-            own_sum[at, :, 0:HD] = grad_keys[rows]
-            own_sum[at, :, HD : 2 * HD] = grad_vals[rows]
-            rows = slice(pairs * pair + BLOCK, (pairs + 1) * pair)
-            to_core[at, :, 0:HD] = grad_keys[rows].astype(BF16)
-            to_core[at, :, HD : 2 * HD] = grad_vals[rows].astype(BF16)
-            sums["core", at] = ship(to_core.at[at], from_core.at[at], at, (0, 0, 1))
+        for index, (half, place, core) in enumerate(blocks_in(first, count)):
+            at = half * ROW + POS[place]
+            rows = slice(index * BLOCK, (index + 1) * BLOCK)
+            if core == 0:
+                own_sum[at, :, 0:HD] = grad_keys[rows]
+                own_sum[at, :, HD : 2 * HD] = grad_vals[rows]
+            else:
+                to_core[at, :, 0:HD] = grad_keys[rows].astype(BF16)
+                to_core[at, :, HD : 2 * HD] = grad_vals[rows].astype(BF16)
+                sums["core", at] = ship(to_core.at[at], from_core.at[at], at, (0, 0, 1))
 
     def chip_total(at):
         sums["core", at].wait_recv()
@@ -304,35 +356,78 @@
             to_owner.at[at], from_owner.at[lands], HALVES * ROW + lands, to
         )
 
+    def neighbour_copy(place):
+        at = ROW + POS[place]
+        first = (POS[ROW - place] - 1) * CORES
+        return term_copy(
+            to_owner.at[at],
+            from_row.at[first + my_core],
+            2 * HALVES * ROW + place,
+            2 * HALVES * ROW + first + my_core,
+            (0, place, speaker),
+        )
+
+    def neighbour_arrived(index):
+        term_copy(
+            from_row.at[index], from_row.at[index], 0, 2 * HALVES * ROW + index, (0, 0, 1)
+        ).wait_recv()
+
+    sibling_copy = term_copy(to_owner.at[ROW], from_row.at[4], 20, 20, (0, 0, 1))
+
+    def opposite_copy(core):
+        return term_copy(
+            to_opposite.at[core],
+            from_owner.at[ROW],
+            21 + core,
+            HALVES * ROW + ROW,
+            (1, 0, (core + 1) % CORES),
+        )
+
     last = pl.ds(far + 3 * pair, pair)
-    middle = pl.ds(far + pair, 2 * pair)
-    prefix_back(far + pair, 2 * pair, grad_probs_of(middle), factors[2])
+    cross = pl.ds(far + 2 * pair, pair)
+    straight = pl.ds(far + pair, pair)
+    prefix_back(far + 2 * pair, pair, grad_probs_of(cross), factors[2])
     prefix_back(far + 3 * pair, pair, grad_probs_of(last), factors[3])
-    send_on(1, 1, (0, 1, 0))
-    send_on(1, 3, (0, 3, 0))
+    prefix_back(far + pair, pair, grad_probs_of(straight), factors[2])
+    for place in (1, 3):
+        at = ROW + POS[place]
+        to_owner[at] = chip_total(at).astype(BF16)
+        neighbour_copy(place).start()
+    send_on(1, 2, (1, 2, 0))
     prefix_back(far, pair, gradp[pl.ds(far, pair), :], factors[1])
-    send_on(1, 2, (1, 2, 0))
     prefix_back(2 * pair, 2 * pair, gradp[pl.ds(2 * pair, 2 * pair), :], factors[0])
+
+    @pl.when(my_core == 0)
+    def _():
+        to_owner[ROW] = chip_total(ROW).astype(BF16)
+        sibling_copy.start()
+
     prefix_back(0, 2 * pair, gradp[pl.ds(0, 2 * pair), :], factors[0])
     send_on(0, 2, (0, 2, 0))
     send_on(0, 3, (0, 3, 0))
     send_on(0, 1, (0, 1, 0))
-
-    total = chip_total(ROW)
-    for place in (1, 3):
-        at = ROW + POS[place]
-        sums["owner", at].wait_recv()
-        total = total + from_owner[at].astype(F32)
-    to_owner[ROW] = total.astype(BF16)
-    sums["owner", ROW] = ship(
-        to_owner.at[ROW], from_owner.at[ROW], HALVES * ROW + ROW, (1, 0, 0)
-    )
-
     grad_keys, grad_vals = back(
         own_rows, own_cols, gradp[own_rows, own_cols], factors[0]
     )
     roll_dkv[0, :, 0:HD] = grad_keys.astype(BF16)
     roll_dkv[0, :, HD : 2 * HD] = grad_vals.astype(BF16)
+
+    @pl.when(my_core == 1)
+    def _():
+        term = chip_total(ROW)
+        for index in (1, 3):
+            neighbour_arrived(index)
+            term = term + from_row[index].astype(F32)
+        to_opposite[1] = term.astype(BF16)
+        opposite_copy(1).start()
+        sibling_copy.wait_recv()
+        term = from_row[4].astype(F32)
+        for index in (0, 2):
+            neighbour_arrived(index)
+            term = term + from_row[index].astype(F32)
+        to_opposite[0] = term.astype(BF16)
+        opposite_copy(0).start()
+
     out = out_t.T
     for head in range(HEADS):
         columns = slice(head * HD, (head + 1) * HD)
@@ -351,12 +446,26 @@
         pre_dq[:, columns] = grad_query[at : at + BLOCK]
 
     total = chip_total(0)
-    for at in (1, 2, 3, ROW + POS[2], ROW):
+    for at in (1, 2, 3, ROW + POS[2]):
         sums["owner", at].wait_recv()
         total = total + from_owner[at].astype(F32)
-    pre_dkv[...] = total.astype(BF16)
-    for copy in (*copies.values(), *sums.values()):
+    opposite_copy(0).wait_recv()
+    pre_dkv[...] = (total + from_owner[ROW].astype(F32)).astype(BF16)
+    for copy in (*copies, *sums.values(), neighbour_copy(1), neighbour_copy(3)):
         copy.wait_send()
+
+    @pl.when(my_core == 0)
+    def _():
+        sibling_copy.wait_send()
+
+    @pl.when(my_core == 1)
+    def _():
+        for core in range(CORES):
+            opposite_copy(core).wait_send()
+            for place in (1, 2, 3):
+                along_row(place, core, start=False)
+            for place in range(ROW):
+                to_sibling(place, core, start=False)
 
 
 def drain(*refs):
@@ -378,8 +487,8 @@
     anywhere = pl.BlockSpec(memory_space=pl.ANY)
     like = lambda array: pltpu.VMEM(array.shape, BF16)
     final = lambda array: jax.ShapeDtypeStruct(array.shape, BF16)
-    copies = GROUP
-    sums = 2 * HALVES * ROW
+    copies = 2 * GROUP
+    sums = 24
     results = pl.pallas_call(
         kernel,
         out_shape=(
@@ -411,6 +520,8 @@
             pltpu.VMEM((HALVES * ROW, BLOCK, 2 * HD), F32),
             pltpu.VMEM((HALVES * ROW, BLOCK, 2 * HD), BF16),
             pltpu.VMEM((HALVES * ROW, BLOCK, 2 * HD), BF16),
+            pltpu.VMEM((5, BLOCK, 2 * HD), BF16),
+            pltpu.VMEM((CORES, BLOCK, 2 * HD), BF16),
             pltpu.SemaphoreType.DMA((6,)),
             pltpu.SemaphoreType.DMA((copies,)),
             pltpu.SemaphoreType.DMA((copies,)),

time: 33.7 us -> 32 us (0.950)
  Pallas kernels: 31.7 us -> 29.9 us
    pallas_call x1, Pallas kernels: 30.7 us -> 29 us  [on_device(): pl.pallas_call(kernel, out_shape=(like(pre_q), like(roll_q), like(pre_q),...]
where the time goes in v4:
time: 32 us; the launch traced here: 31.8 us
  Pallas kernels  29.9 us (93%)
  between operations  1.93 us (6%)
    pallas_call x1, Pallas kernels, on_device(): pl.pallas_call(kernel, out_shape=(like(pre_q), like(roll_q), like(pre_q),...  29 us
    pallas_call x1, Pallas kernels, on_device(): pl.pallas_call(drain, out_shape=tuple((final(array) for array in (pre_q,...  0.95 us

profile of v4, /device:TPU:1, one launch (start us, length us, event | category | flops | bytes accessed | tf_op | source)
XLA Modules:
  0.0 31.8 jit_solution(4264072706532182343)
XLA Ops:
  1.9 29.0 %shard_map.127 = (bf16[64,1024]{1,0:T(8,128)(2,1)S(1)}, bf16[1,128,1024]{2,1,0:T(8,128)(2,1)S(1)}, bf16[64,1024]{1,0:T(8,128)(2,1)S(1)}, bf16[1,128,1024]{2,1,0:...) custom-call(s32[1]{0:T(128)S(6)} %copy.14.pre_len_ref, s32[1]{0:T(128)S(6)} %copy.15.roll_len_ref, ...), custom_call_target="tpu_custom_call" | custom-call | tf_op jit(solution)/shard_map/pallas_call | solution.py:492
  30.9 1.0 %shard_map.128 = (bf16[64,1024]{1,0:T(8,128)(2,1)}, bf16[1,128,1024]{2,1,0:T(8,128)(2,1)}, bf16[64,1024]{1,0:T(8,128)(2,1)}, bf16[1,128,1024]{2,1,0:T(8,128)(2,1...) custom-call(bf16[64,1024]{1,0:T(8,128)(2,1)S(1)} %get-tuple-element.12.refs_0_, ...), custom_call_target="tpu_custom_call" | custom-call | tf_op jit(solution)/shard_map/pallas_call | solution.py:535

commit v5 on v4

--- a/solution.py
+++ b/solution.py
@@ -103,7 +103,7 @@
         )
 
     speaker = 1 - my_core
-    partners = [(1, 0, speaker), (0, 0, 1), (0, 1, 0), (0, 3, 0), (0, 2, 0)]
+    partners = [(0, 0, 1), (0, 1, 0), (0, 3, 0), (0, 2, 0)]
     barrier = pltpu.get_barrier_semaphore()
 
     def announce(partner):
@@ -111,12 +111,13 @@
             barrier, inc=1, device_id={"roll": device(*partner)}, device_id_type=MESH
         )
 
+    @pl.when(my_core == 1)
+    def _():
+        announce((1, 0, 0))
+        announce((1, 0, 1))
+
     for partner in partners:
         announce(partner)
-
-    @pl.when(my_core == 1)
-    def _():
-        announce((1, 0, 1))
 
     loads = []
     for index, (source, target) in enumerate(
@@ -167,7 +168,7 @@
 
     copies = []
     loads[0].wait()
-    pl.semaphore_wait(barrier, len(partners) + my_core)
+    pl.semaphore_wait(barrier, len(partners) + 1)
     held = kvs.at[rows_of(0, 0, 0)]
     copies.append(push(held, slot(1, 0, 0) + speaker, 0, (1, 0, speaker)))
     for place in (2, 1, 3):
@@ -247,11 +248,11 @@
     def _():
         for core in range(CORES):
             arrived(1, 0, core)
-        for place in (2, 1, 3):
+        for core in range(CORES):
+            to_sibling(0, core)
+        for place in (1, 3, 2):
             for core in range(CORES):
                 along_row(place, core)
-        for core in range(CORES):
-            to_sibling(0, core)
 
     for place in (1, 3, 2):
         arrived(0, place, 1)

time: 32 us -> 31.2 us (0.975)
  Pallas kernels: 29.9 us -> 29.2 us
    pallas_call x1, Pallas kernels: 29 us -> 28.2 us  [on_device(): pl.pallas_call(kernel, out_shape=(like(pre_q), like(roll_q), like(pre_q),...]
where the time goes in v5:
time: 31.2 us; the launch traced here: 31.1 us
  Pallas kernels  29.2 us (94%)
  between operations  1.93 us (6%)
    pallas_call x1, Pallas kernels, on_device(): pl.pallas_call(kernel, out_shape=(like(pre_q), like(roll_q), like(pre_q),...  28.2 us
    pallas_call x1, Pallas kernels, on_device(): pl.pallas_call(drain, out_shape=tuple((final(array) for array in (pre_q,...  0.95 us

profile of v5, /device:TPU:1, one launch (start us, length us, event | category | flops | bytes accessed | tf_op | source)
XLA Modules:
  0.0 31.1 jit_solution(14921934874879582834)
XLA Ops:
  1.9 28.2 %shard_map.127 = (bf16[64,1024]{1,0:T(8,128)(2,1)S(1)}, bf16[1,128,1024]{2,1,0:T(8,128)(2,1)S(1)}, bf16[64,1024]{1,0:T(8,128)(2,1)S(1)}, bf16[1,128,1024]{2,1,0:...) custom-call(s32[1]{0:T(128)S(6)} %copy.14.pre_len_ref, s32[1]{0:T(128)S(6)} %copy.15.roll_len_ref, ...), custom_call_target="tpu_custom_call" | custom-call | tf_op jit(solution)/shard_map/pallas_call | solution.py:493
  30.2 1.0 %shard_map.128 = (bf16[64,1024]{1,0:T(8,128)(2,1)}, bf16[1,128,1024]{2,1,0:T(8,128)(2,1)}, bf16[64,1024]{1,0:T(8,128)(2,1)}, bf16[1,128,1024]{2,1,0:T(8,128)(2,1...) custom-call(bf16[64,1024]{1,0:T(8,128)(2,1)S(1)} %get-tuple-element.12.refs_0_, ...), custom_call_target="tpu_custom_call" | custom-call | tf_op jit(solution)/shard_map/pallas_call | solution.py:536

commit v6 on v5

--- a/solution.py
+++ b/solution.py
@@ -203,7 +203,6 @@
 
     def take(first, count):
         at = pl.ds(first, count)
-        keys_t[:, at] = kvs[at, 0:HD].T
         vals_t[:, at] = kvs[at, HD : 2 * HD].T
         row = lax.broadcasted_iota(jnp.int32, (count, 1), 0)
         base = 0
@@ -232,7 +231,6 @@
     own_logits = jnp.where(own_key <= own_limit, own_logits, masked_score)
     score[own_rows, own_cols] = own_logits
     own_max = fold8(own_logits, jnp.max)
-    keys_t[:, own_rows] = rkv[:, 0:HD].T
     vals_t[:, own_rows] = rkv[:, HD : 2 * HD].T
     gradp[own_rows, own_cols] = dot(rkv[:, HD : 2 * HD], grads[own_cols, :], 1, 1)
     grad_t = grads[...].T.astype(F32)
@@ -435,6 +433,8 @@
         roll_out[0, :, columns] = out[head * RESP : (head + 1) * RESP]
         at = ROLL_ROWS + head * BLOCK
         pre_out[:, columns] = out[at : at + BLOCK]
+    keys_t[:, 0:PREFIX] = kvs[:, 0:HD].T
+    keys_t[:, own_rows] = rkv[:, 0:HD].T
     grad_query = dot(keys_t[:, 0:PREFIX], weight[0:PREFIX, :], 1, 0)
     grad_query = widen(
         grad_query, dot(keys_t[:, own_rows], weight[own_rows, own_cols], 1, 0), jnp.add

time: 31.2 us -> 31.2 us (level)
  no operation moved by 1% of the time
where the time goes in v6:
time: 31.2 us; the launch traced here: 31.1 us
  Pallas kernels  29.2 us (94%)
  between operations  1.93 us (6%)
    pallas_call x1, Pallas kernels, on_device(): pl.pallas_call(kernel, out_shape=(like(pre_q), like(roll_q), like(pre_q),...  28.2 us
    pallas_call x1, Pallas kernels, on_device(): pl.pallas_call(drain, out_shape=tuple((final(array) for array in (pre_q,...  0.95 us

profile of v6, /device:TPU:1, one launch (start us, length us, event | category | flops | bytes accessed | tf_op | source)
XLA Modules:
  0.0 31.1 jit_solution(2138213780132398352)
XLA Ops:
  1.9 28.2 %shard_map.127 = (bf16[64,1024]{1,0:T(8,128)(2,1)S(1)}, bf16[1,128,1024]{2,1,0:T(8,128)(2,1)S(1)}, bf16[64,1024]{1,0:T(8,128)(2,1)S(1)}, bf16[1,128,1024]{2,1,0:...) custom-call(s32[1]{0:T(128)S(6)} %copy.14.pre_len_ref, s32[1]{0:T(128)S(6)} %copy.15.roll_len_ref, ...), custom_call_target="tpu_custom_call" | custom-call | tf_op jit(solution)/shard_map/pallas_call | solution.py:493
  30.2 1.0 %shard_map.128 = (bf16[64,1024]{1,0:T(8,128)(2,1)}, bf16[1,128,1024]{2,1,0:T(8,128)(2,1)}, bf16[64,1024]{1,0:T(8,128)(2,1)}, bf16[1,128,1024]{2,1,0:T(8,128)(2,1...) custom-call(bf16[64,1024]{1,0:T(8,128)(2,1)S(1)} %get-tuple-element.12.refs_0_, ...), custom_call_target="tpu_custom_call" | custom-call | tf_op jit(solution)/shard_map/pallas_call | solution.py:536

commit v7 on v6

--- a/solution.py
+++ b/solution.py
@@ -246,11 +246,12 @@
     def _():
         for core in range(CORES):
             arrived(1, 0, core)
+        for place in (1, 3):
+            for core in range(CORES):
+                along_row(place, core)
         for core in range(CORES):
             to_sibling(0, core)
-        for place in (1, 3, 2):
-            for core in range(CORES):
-                along_row(place, core)
+            along_row(2, core)
 
     for place in (1, 3, 2):
         arrived(0, place, 1)

time: 31.2 us -> 31.2 us (level)
  no operation moved by 1% of the time
where the time goes in v7:
time: 31.2 us; the launch traced here: 31.1 us
  Pallas kernels  29.2 us (94%)
  between operations  1.93 us (6%)
    pallas_call x1, Pallas kernels, on_device(): pl.pallas_call(kernel, out_shape=(like(pre_q), like(roll_q), like(pre_q),...  28.2 us
    pallas_call x1, Pallas kernels, on_device(): pl.pallas_call(drain, out_shape=tuple((final(array) for array in (pre_q,...  0.95 us

profile of v7, /device:TPU:1, one launch (start us, length us, event | category | flops | bytes accessed | tf_op | source)
XLA Modules:
  0.0 31.1 jit_solution(2075839899404019992)
XLA Ops:
  1.9 28.2 %shard_map.127 = (bf16[64,1024]{1,0:T(8,128)(2,1)S(1)}, bf16[1,128,1024]{2,1,0:T(8,128)(2,1)S(1)}, bf16[64,1024]{1,0:T(8,128)(2,1)S(1)}, bf16[1,128,1024]{2,1,0:...) custom-call(s32[1]{0:T(128)S(6)} %copy.14.pre_len_ref, s32[1]{0:T(128)S(6)} %copy.15.roll_len_ref, ...), custom_call_target="tpu_custom_call" | custom-call | tf_op jit(solution)/shard_map/pallas_call | solution.py:494
  30.2 1.0 %shard_map.128 = (bf16[64,1024]{1,0:T(8,128)(2,1)}, bf16[1,128,1024]{2,1,0:T(8,128)(2,1)}, bf16[64,1024]{1,0:T(8,128)(2,1)}, bf16[1,128,1024]{2,1,0:T(8,128)(2,1...) custom-call(bf16[64,1024]{1,0:T(8,128)(2,1)S(1)} %get-tuple-element.12.refs_0_, ...), custom_call_target="tpu_custom_call" | custom-call | tf_op jit(solution)/shard_map/pallas_call | solution.py:537
